TPU v7x, 128 devices: a whole 4x4x4 slice. The times are simulated.
128 devices in a mesh: role: 2 (over core), dev: 64 (over x, y, z).
Axes of the slice: x: 4, y: 4, z: 4, core: 2. Of those that a mesh axis runs over, the one named last changes fastest.
Arguments:
- tokens: bfloat16 [16384, 3584], P(('role', 'dev')), may hold values from -6 to 6
- grad_out: bfloat16 [16384, 3584], P(('role', 'dev')), may hold values from -6 to 6
- routes: int32 [16384, 4], P(('role', 'dev')), may hold values from 0 to 127, all different within a row; in each aligned block of 128 rows (0 to 127, 128 to 255, ...) at most 5 rows name the same one
- gates: float32 [16384, 4], P(('role', 'dev')), may hold values from 0.1 to 0.8
- gate_weight: bfloat16 [128, 3584, 1024], P(('role', 'dev')), may hold values from -0.09375 to 0.09375
- up_weight: bfloat16 [128, 3584, 1024], P(('role', 'dev')), may hold values from -0.09375 to 0.09375
- down_weight: bfloat16 [128, 1024, 3584], P(('role', 'dev')), may hold values from -0.1875 to 0.1875
Outputs:
- layer_out: bfloat16 [16384, 3584], P(('role', 'dev'))
- grad_in: bfloat16 [16384, 3584], P(('role', 'dev'))
Inputs may be any that keep to these rules, and one draw needn't show every extreme that they name: `routes`: within the 4 entries of a token the experts differ. In the rows of one device (aligned blocks of 128 tokens) no expert is named more than 5 times, a bound that some block reaches.
All inputs are finite; a program needn't handle non-finite values.
Results may differ from a plain program's by a relative error of at most 0.006.
Values may be sent and summed in bfloat16 or wider, within the bound.
No kernel may reach another device: no remote copies, remote signals or barrier semaphores. Data moves between devices by JAX's collectives and lax.ppermute only.
A program may use at most 128 MiB of HBM per device.

v0:
```python
import jax
import jax.numpy as jnp
from jax import lax
from jax.sharding import PartitionSpec as P

epsilon = 1e-06


def expert_rows(stacked, gate_weight, up_weight, down_weight):
    normed = stacked[:, 0]
    grad_scaled = stacked[:, 1]
    hidden_a = jnp.dot(normed, gate_weight, preferred_element_type=jnp.float32)
    hidden_b = jnp.dot(normed, up_weight, preferred_element_type=jnp.float32)
    sigmoid_a = jax.nn.sigmoid(hidden_a)
    silu_a = hidden_a * sigmoid_a
    product = (silu_a * hidden_b).astype(jnp.bfloat16)
    expert_out = jnp.dot(product, down_weight, preferred_element_type=jnp.float32).astype(
        jnp.bfloat16
    )
    contract = (((1,), (1,)), ((), ()))
    grad_act = lax.dot_general(
        grad_scaled, down_weight, contract, preferred_element_type=jnp.float32
    )
    silu_slope = sigmoid_a * (1.0 + hidden_a * (1.0 - sigmoid_a))
    grad_a = (grad_act * hidden_b * silu_slope).astype(jnp.bfloat16)
    grad_b = (grad_act * silu_a).astype(jnp.bfloat16)
    grad_rows = lax.dot_general(grad_a, gate_weight, contract, preferred_element_type=jnp.float32)
    grad_rows = grad_rows + lax.dot_general(
        grad_b, up_weight, contract, preferred_element_type=jnp.float32
    )
    return jnp.stack([expert_out, grad_rows.astype(jnp.bfloat16)], axis=1)


def local(tokens, grad_out, routes, gates, gate_weight, up_weight, down_weight):
    tok_rows, features = tokens.shape
    top_count = routes.shape[1]
    role_count = lax.axis_size("role")
    experts = role_count * lax.axis_size("dev")
    capacity = tok_rows * top_count * 5 // (4 * experts)
    tokens_wide = tokens.astype(jnp.float32)
    inv_rms = lax.rsqrt(jnp.mean(tokens_wide * tokens_wide, axis=1, keepdims=True) + epsilon)
    normed = (tokens_wide * inv_rms).astype(jnp.bfloat16)
    grad_scaled = (gates[:, :, None] * grad_out.astype(jnp.float32)[:, None, :]).astype(
        jnp.bfloat16
    )
    stacked = jnp.stack(
        [jnp.broadcast_to(normed[:, None, :], grad_scaled.shape), grad_scaled], axis=2
    )
    stacked = stacked.reshape(tok_rows * top_count, 2, features)
    flat_routes = routes.reshape(-1)
    one_hot = (flat_routes[:, None] == jnp.arange(experts, dtype=jnp.int32)[None, :]).astype(
        jnp.int32
    )
    earlier = jnp.cumsum(one_hot, axis=0) - one_hot
    places = flat_routes * capacity + jnp.sum(earlier * one_hot, axis=1)
    buffer = jnp.zeros((experts * capacity, 2, features), jnp.bfloat16).at[places].set(stacked)
    gate_local = gate_weight[0]
    up_local = up_weight[0]
    down_local = down_weight[0]
    arrived = lax.all_to_all(
        buffer.reshape(experts, capacity, 2, features),
        ("role", "dev"),
        split_axis=0,
        concat_axis=0,
        tiled=True,
    )
    slot_count = arrived.shape[1]
    result = expert_rows(arrived.reshape(-1, 2, features), gate_local, up_local, down_local)
    result = result.reshape(experts, slot_count, 2, features)
    returned = lax.all_to_all(result, ("role", "dev"), split_axis=0, concat_axis=0, tiled=True)
    picked = returned.reshape(experts * capacity, 2, features)[places]
    picked = picked.reshape(tok_rows, top_count, 2, features).astype(jnp.float32)
    expert_sum = jnp.sum(gates[:, :, None] * picked[:, :, 0], axis=1)
    layer_out = (tokens_wide + expert_sum).astype(jnp.bfloat16)
    grad_normed = jnp.sum(picked[:, :, 1], axis=1)
    projected = jnp.mean(grad_normed * tokens_wide, axis=1, keepdims=True)
    grad_in = (
        grad_out.astype(jnp.float32) + inv_rms * grad_normed - tokens_wide * inv_rms**3 * projected
    )
    return (layer_out, grad_in.astype(jnp.bfloat16))


def solution(mesh):
    in_specs = (
        P(("role", "dev"), None),
        P(("role", "dev"), None),
        P(("role", "dev"), None),
        P(("role", "dev"), None),
        P(("role", "dev"), None, None),
        P(("role", "dev"), None, None),
        P(("role", "dev"), None, None),
    )
    out_specs = (P(("role", "dev"), None), P(("role", "dev"), None))
    return jax.shard_map(local, mesh=mesh, in_specs=in_specs, out_specs=out_specs, check_vma=False)
```

profile of v0, /device:TPU:13, one launch (start us, length us, event | category | flops | bytes accessed | tf_op | source)
XLA Modules:
  0.0 618.5 jit_solution(4021286455803592526)
XLA Ops:
  0.6 0.8 copy.29
  1.6 0.7 broadcast_multiply_fusion
  3.0 1.4 fusion.23
  5.0 1.4 fusion.24
  6.4 2.8 stack_broadcast_in_dim.7
  9.1 6.8 %stack_broadcast_in_dim.8 = bf16[512,1,3584]{2,0,1:T(8,128)(2,1)} reshape(bf16[128,4,3584]{2,1,0:T(4,128)(2,1)} %stack_broadcast_in_dim.7) | data formatting | bytes 7340032 | tf_op jit(solution)/shard_map/stack;broadcast_in_dim | solution.py:46
  16.2 3.9 mul.119
  20.2 9.0 %mul.120 = f32[512,1,3584]{2,0,1:T(8,128)} reshape(f32[128,4,3584]{2,1,0:T(4,128)} %mul.119) | data formatting | bytes 14680064 | tf_op jit(solution)/shard_map/mul | solution.py:43
  29.2 6.1 multiply_convert_fusion
  35.3 2.7 pad_maximum_fusion.1
  38.0 40.8 %copy.34 = bf16[512,2,3584]{2,1,0:T(2,128)(2,1)} copy(bf16[512,2,3584]{2,0,1:T(8,128)(2,1)S(1)} %pad_maximum_fusion.1) | data formatting | bytes 14680064 | tf_op jit(solution)/shard_map/stack | solution.py:46
  79.0 6.0 broadcast_in_dim.2
  85.0 67.1 %scatter_fusion = bf16[640,2,3584]{2,1,0:T(2,128)(2,1)} fusion(bf16[640,2,3584]{2,1,0:T(2,128)(2,1)} %broadcast_in_dim.2, s32[512]{0:T(512)S(1)} %bitcast.56, bf16[512,2,3584]{2,1,0:T(2,128)(2,1)} %copy.34), kind=kCustom, calls=%fused_computation.1 | custom fusion | bytes 22022144 | tf_op jit(solution)/shard_map/scatter | solution.py:56
  152.1 139.2 %all_to_all.10 = bf16[128,5,2,3584]{3,2,1,0:T(2,128)(2,1)S(1)} all-to-all(bf16[128,5,2,3584]{3,2,1,0:T(2,128)(2,1)} %bitcast.53), channel_id=1, replica_groups=mesh['role'=2,'dev'=64] {'role','dev'}, dimensions={0} | all-to-all | bytes 18350080 | tf_op jit(solution)/shard_map/all_to_all | solution.py:60
  291.3 13.7 %fusion.43 = (bf16[640,1,3584]{2,1,0:T(2,128)(2,1)}, bf16[640,1,3584]{2,1,0:T(2,128)(2,1)S(1)}) fusion(bf16[640,2,3584]{2,1,0:T(2,128)(2,1)S(1)} %bitcast.52), kind=kLoop, calls=%fused_computation.66 | loop fusion | bytes 18350080 | tf_op jit(solution)/shard_map/slice | solution.py:10
  305.0 9.8 %fusion.11 = f32[640,1024]{1,0:T(8,128)S(1)} fusion(bf16[1,3584,1024]{2,1,0:T(8,128)(2,1)} %param.11, bf16[640,1,3584]{2,1,0:T(2,128)(2,1)} %get-tuple-element.4), kind=kOutput, calls=%fused_computation.18 | convolution fusion | flops 4697620480 | bytes 14548992 | tf_op jit(solution)/shard_map/dot_general | solution.py:12
  314.8 8.6 %fusion.7 = f32[640,1024]{1,0:T(8,128)} fusion(bf16[1,3584,1024]{2,1,0:T(8,128)(2,1)} %param.12, bf16[640,1,3584]{2,1,0:T(2,128)(2,1)S(1)} %copy-done.2), kind=kOutput, calls=%fused_computation.14 | convolution fusion | flops 4697620480 | bytes 14548992 | tf_op jit(solution)/shard_map/dot_general | solution.py:13
  323.5 7.2 %fusion.1 = f32[640,1024]{1,0:T(8,128)S(1)} fusion(bf16[1,1024,3584]{2,1,0:T(8,128)(2,1)} %param.13, bf16[640,1,3584]{2,1,0:T(2,128)(2,1)S(1)} %get-tuple-element.5), kind=kOutput, calls=%fused_computation.8 | convolution fusion | flops 4697620480 | bytes 14548992 | tf_op jit(solution)/shard_map/dot_general | solution.py:21
  330.7 11.5 %fusion.5 = f32[640,3584]{1,0:T(8,128)} fusion(bf16[1,3584,1024]{2,1,0:T(8,128)(2,1)} %param.12, f32[640,1024]{1,0:T(8,128)S(1)} %fusion.1, f32[640,1024]{1,0:T(8,128)S(1)} %fusion.11), kind=kOutput, calls=%fused_computation.12 | convolution fusion | flops 4701552640 | bytes 21757952 | tf_op jit(solution)/shard_map/dot_general | solution.py:28
  342.2 10.3 %fusion.13 = bf16[640,3584]{1,0:T(8,128)(2,1)} fusion(bf16[1,1024,3584]{2,1,0:T(8,128)(2,1)} %param.13, f32[640,1024]{1,0:T(8,128)S(1)} %copy-done.12, f32[640,1024]{1,0:T(8,128)S(1)} %fusion.11), kind=kOutput, calls=%fused_computation.21 | convolution fusion | flops 4703846400 | bytes 17170432 | tf_op jit(solution)/shard_map/dot_general | solution.py:17
  352.4 14.8 %add_convert_fusion = bf16[640,3584]{1,0:T(8,128)(2,1)} fusion(f32[640,3584]{1,0:T(8,128)} %fusion.5, bf16[1,3584,1024]{2,1,0:T(8,128)(2,1)} %param.11, f32[640,1024]{1,0:T(8,128)S(1)} %fusion.11, f32[640,1024]{1,0:T(8,128)} %copy-done.11, f32[640,1024]{1,0:T(8,128)} %fusion.7), kind=kOutput, calls=%fused_computation.3 | convolution fusion | flops 4708761600 | bytes 28966912 | tf_op jit(solution)/shard_map/dot_general | solution.py:27
  367.2 7.9 %stack.15 = bf16[128,5,1,3584]{3,1,0,2:T(8,128)(2,1)} reshape(bf16[640,3584]{1,0:T(8,128)(2,1)} %add_convert_fusion) | data formatting | bytes 9175040 | tf_op jit(solution)/shard_map/stack | solution.py:31
  375.1 7.9 %stack.14 = bf16[128,5,1,3584]{3,1,0,2:T(8,128)(2,1)} reshape(bf16[640,3584]{1,0:T(8,128)(2,1)} %fusion.13) | data formatting | bytes 9175040 | tf_op jit(solution)/shard_map/stack | solution.py:31
  383.0 8.6 %pad_maximum_fusion = bf16[128,5,2,3584]{3,1,0,2:T(8,128)(2,1)S(1)} fusion(bf16[128,5,1,3584]{3,1,0,2:T(8,128)(2,1)} %stack.15, bf16[128,5,1,3584]{3,1,0,2:T(8,128)(2,1)} %stack.14), kind=kLoop, calls=%fused_computation.2 | loop fusion | flops 4587520 | bytes 18350080 | tf_op jit(solution)/shard_map/stack | solution.py:31
  391.6 9.8 %copy.35 = bf16[128,5,2,3584]{3,2,1,0:T(2,128)(2,1)} copy(bf16[128,5,2,3584]{3,1,0,2:T(8,128)(2,1)S(1)} %pad_maximum_fusion) | data formatting | bytes 18350080 | tf_op jit(solution)/shard_map/stack | solution.py:31
  401.4 6.8 %all-to-all-start.1 = ((bf16[128,5,2,3584]{3,2,1,0:T(2,128)(2,1)}), bf16[128,5,2,3584]{3,2,1,0:T(2,128)(2,1)}, u32[]{:S(2)}, u32[]{:S(2)}) async-start(bf16[128,5,2,3584]{3,2,1,0:T(2,128)(2,1)} %copy.35), calls=%async_computation.1 | async-start | bytes 18350080 | tf_op jit(solution)/shard_map/all_to_all | solution.py:70
  408.2 138.3 %all-to-all-done.1 = bf16[128,5,2,3584]{3,2,1,0:T(2,128)(2,1)} async-done(((bf16[128,5,2,3584]{3,2,1,0:T(2,128)(2,1)}), bf16[128,5,2,3584]{3,2,1,0:T(2,128)(2,1)}, u32[]{:S(2)}, u32[]{:S(2)}) %all-to-all-start.1) | async-done | bytes 9175072 | tf_op jit(solution)/shard_map/all_to_all | solution.py:70
  546.5 29.3 %gather_fusion = bf16[512,2,3584]{2,1,0:T(2,128)(2,1)} fusion(bf16[640,2,3584]{2,1,0:T(2,128)(2,1)} %bitcast.10, s32[1024]{0:T(1024)S(1)} %pad_clamp_fusion), kind=kCustom, calls=%fused_computation | custom fusion | bytes 14682112 | tf_op jit(solution)/shard_map/gather | solution.py:71
  575.8 10.6 %bitcast_convert_fusion = f32[128,4,2,3584]{3,2,1,0:T(2,128)} fusion(bf16[512,2,3584]{2,1,0:T(2,128)(2,1)} %gather_fusion), kind=kLoop, calls=%fused_computation.62 | loop fusion | flops 3670016 | bytes 22020096 | tf_op jit(solution)/shard_map/convert_element_type | solution.py:72
  586.5 20.4 %slice_reduce_fusion = (f32[128,3584]{1,0:T(8,128)S(1)}, f32[128,4,1,3584]{3,2,1,0:T(1,128)}) fusion(f32[128,4,2,3584]{3,2,1,0:T(2,128)} %bitcast_convert_fusion), kind=kLoop, calls=%fused_computation.4 | loop fusion | flops 1376256 | bytes 23855104 | tf_op jit(solution)/shard_map/reduce_sum | solution.py:75
  606.9 8.8 %fusion = f32[128,3584]{1,0:T(8,128)S(1)} fusion(f32[128,4,1,3584]{3,2,1,0:T(1,128)} %get-tuple-element.3, f32[128,4]{1,0:T(8,128)S(1)} %copy-done.6), kind=kLoop, calls=%fused_computation.7 | loop fusion | flops 3211264 | bytes 9177088 | tf_op jit(solution)/shard_map/reduce_sum | solution.py:73
  616.1 2.2 fusion.28
  (46 shorter events, 2.2 us)
Async XLA Ops:
  5.0 1.4 copy-start.8
  9.1 6.8 %copy-start.7 = (f32[128,4]{0,1:T(4,128)S(1)}, f32[128,4]{0,1:T(4,128)}, u32[]{:S(2)}) copy-start(f32[128,4]{0,1:T(4,128)} %param.10) | copy-start | bytes 6148
  9.1 7.1 %copy-start.3 = (bf16[128,3584]{1,0:T(8,128)(2,1)S(1)}, bf16[128,3584]{1,0:T(8,128)(2,1)}, u32[]{:S(2)}) copy-start(bf16[128,3584]{1,0:T(8,128)(2,1)} %param.8) | copy-start | bytes 2752516
  16.1 4.1 copy-start.5
  29.2 6.1 copy-start
  305.0 9.8 %copy-start.2 = (bf16[640,1,3584]{2,1,0:T(2,128)(2,1)S(1)}, bf16[640,1,3584]{2,1,0:T(2,128)(2,1)}, u32[]{:S(2)}) copy-start(bf16[640,1,3584]{2,1,0:T(2,128)(2,1)} %get-tuple-element.4) | copy-start | bytes 13762564
  330.7 11.5 %copy-start.11 = (f32[640,1024]{1,0:T(8,128)}, f32[640,1024]{1,0:T(8,128)S(1)}, u32[]{:S(2)}) copy-start(f32[640,1024]{1,0:T(8,128)S(1)} %fusion.1) | copy-start | bytes 7864324
  330.7 11.5 %copy-start.12 = (f32[640,1024]{1,0:T(8,128)S(1)}, f32[640,1024]{1,0:T(8,128)}, u32[]{:S(2)}) copy-start(f32[640,1024]{1,0:T(8,128)} %fusion.7) | copy-start | bytes 7864324
  401.4 145.2 %all-to-all-start.1 = ((bf16[128,5,2,3584]{3,2,1,0:T(2,128)(2,1)}), bf16[128,5,2,3584]{3,2,1,0:T(2,128)(2,1)}, u32[]{:S(2)}, u32[]{:S(2)}) async-start(bf16[128,5,2,3584]{3,2,1,0:T(2,128)(2,1)} %copy.35), calls=%async_computation.1 | async-start | bytes 18350080 | tf_op jit(solution)/shard_map/all_to_all | solution.py:70
  586.5 20.4 %copy-start.6 = (f32[128,4]{1,0:T(8,128)S(1)}, f32[128,4]{1,0:T(8,128)}, u32[]{:S(2)}) copy-start(f32[128,4]{1,0:T(8,128)} %copy-done.5) | copy-start | bytes 6148
  606.9 8.9 %copy-start.1 = (bf16[128,3584]{1,0:T(8,128)(2,1)S(1)}, bf16[128,3584]{1,0:T(8,128)(2,1)}, u32[]{:S(2)}) copy-start(bf16[128,3584]{1,0:T(8,128)(2,1)} %param.7) | copy-start | bytes 2752516
  606.9 9.2 %copy-start.4 = (bf16[128,3584]{1,0:T(8,128)(2,1)S(1)}, bf16[128,3584]{1,0:T(8,128)(2,1)}, u32[]{:S(2)}) copy-start(bf16[128,3584]{1,0:T(8,128)(2,1)} %param.8) | copy-start | bytes 2752516
  606.9 9.2 %copy-start.9 = (f32[128]{0:T(128)S(1)}, f32[128]{0:T(128)}, u32[]{:S(2)}) copy-start(f32[128]{0:T(128)} %copy-done.8) | copy-start | bytes 1540
  606.9 9.2 %copy-start.10 = (f32[128]{0:T(128)S(1)}, f32[128]{0:T(128)}, u32[]{:S(2)}) copy-start(f32[128]{0:T(128)} %get-tuple-element.8) | copy-start | bytes 1540
where the time goes:
time: 628 us; the launch traced here: 619 us
  local copies, waits for them, and re-layouts  207 us (33%)
  blocking collectives  139 us (22%)
  waiting for transfers between devices  138 us (22%)
  other arithmetic  64.3 us (10%)
  matrix products  62.1 us (10%)
  starting transfers between devices  6.82 us (1%)
    all_to_all x1, blocking collectives, local(): lax.all_to_all(buffer.reshape(experts, capacity, 2, features), ('role', '...  139 us
    all_to_all x1, waiting for transfers between devices, local(): lax.all_to_all(result, ('role', 'dev'), split_axis=0, concat_axis=0, tile...  138 us
    scatter x1, local copies, waits for them, and re-layouts, local(): jnp.zeros((experts * capacity, 2, features), jnp.bfloat16).at[places]  67.1 us
    another operation x3, local copies, waits for them, and re-layouts, local(): jnp.stack([jnp.broadcast_to(normed[:, None, :], grad_scaled.shape), grad_...  50.4 us
    gather x1, local copies, waits for them, and re-layouts, local(): picked = returned.reshape(experts * capacity, 2, features)[places]  29.3 us
    another operation x3, local copies, waits for them, and re-layouts, expert_rows(): return jnp.stack([expert_out, grad_rows.astype(jnp.bfloat16)], axis=1)  25.5 us
    reduce_sum x1, other arithmetic, local(): grad_normed = jnp.sum(picked[:, :, 1], axis=1)  20.4 us
    dot_general x1, matrix products, expert_rows(): lax.dot_general(grad_a, gate_weight, contract, preferred_element_type=jnp...  14.8 us
  transfers between devices with their start and end apart: 1, of which 1 were waited for; matrix products, arithmetic and copies ran while one was open for 0% of the time, Pallas kernels for 0%

commit v1 on v0

v1 whole, which is shorter than its diff:
```python
import jax
import jax.numpy as jnp
import numpy as np
from jax import lax
from jax.experimental import pallas as pl
from jax.experimental.pallas import tpu as pltpu
from jax.sharding import PartitionSpec as P

epsilon = 1e-06
bf16, f32 = jnp.bfloat16, jnp.float32
CHUNKS = 4
BLOCK = 64
VMEM_LIMIT = 60 * 1024 * 1024


def dot(a, b):
    return jnp.dot(a, b, preferred_element_type=f32)


def dot_nt(a, b):
    return lax.dot_general(a, b, (((1,), (1,)), ((), ())), preferred_element_type=f32)


def permutation(to_wire):
    size = BLOCK * CHUNKS
    wire = lax.broadcasted_iota(jnp.int32, (size, size), 0 if to_wire else 1)
    held = lax.broadcasted_iota(jnp.int32, (size, size), 1 if to_wire else 0)
    return jnp.where((wire & (CHUNKS - 1)) * BLOCK + wire // CHUNKS == held, 1.0, 0.0).astype(bf16)


def to_wire(perm, rows, width):
    stacked = jnp.concatenate([rows[:, c * width : (c + 1) * width] for c in range(CHUNKS)], axis=0)
    return dot(perm, stacked).astype(bf16)


def route_kernel(role_ref, own_ref, partner_ref, expand_ref, target_ref, p_ref, pt_ref, gate_ref, hi_ref, lo_ref):
    experts = expand_ref.shape[1]
    rows = own_ref.shape[1]
    named = lax.broadcasted_iota(jnp.int32, (experts, rows), 0) + role_ref[0] * experts
    named = named.astype(f32)
    before = lax.broadcasted_iota(jnp.int32, (rows, rows), 0)
    after = lax.broadcasted_iota(jnp.int32, (rows, rows), 1)
    strict = jnp.where(before < after, 1.0, 0.0).astype(bf16)
    ranks, gates = [], []
    for ref in (own_ref, partner_ref):
        top = ref.shape[0] // 2
        uses = jnp.zeros((experts, rows), f32)
        gate = jnp.zeros((experts, rows), f32)
        for k in range(top):
            hit = named == ref[k : k + 1, :]
            uses = jnp.where(hit, 1.0, uses)
            gate = jnp.where(hit, ref[top + k : top + k + 1, :], gate)
        ranks.append(uses * (dot(uses.astype(bf16), strict) + 1.0))
        gates.append(gate)
    expand = expand_ref[...]
    rank = jnp.concatenate(ranks, axis=1).astype(bf16)
    gate = jnp.concatenate(gates, axis=1)
    chosen = dot(expand, rank) == target_ref[...].astype(f32)
    first = gate.astype(bf16)
    rest = gate - first.astype(f32)
    second = rest.astype(bf16)
    third = (rest - second.astype(f32)).astype(bf16)
    spread = dot(expand, first) + (dot(expand, second) + dot(expand, third))
    spread = jnp.where(chosen, spread, 0.0)
    one_hot = jnp.where(chosen, 1.0, 0.0)
    p_ref[...] = one_hot.astype(bf16)
    pt_ref[...] = jnp.transpose(one_hot).astype(bf16)
    gate_ref[...] = jnp.sum(spread, axis=1, keepdims=True)
    turned = jnp.transpose(spread)
    hi = turned.astype(bf16)
    hi_ref[...] = hi
    lo_ref[...] = (turned - hi.astype(f32)).astype(bf16)


def pack_normed_kernel(p_ref, own_ref, partner_ref, out_ref, normed_ref):
    rows, features = own_ref.shape

    @pl.when(pl.program_id(0) == 0)
    def _():
        for i, ref in enumerate((own_ref, partner_ref)):
            wide = ref[...].astype(f32)
            inv_rms = lax.rsqrt(jnp.mean(wide * wide, axis=1, keepdims=True) + epsilon)
            normed_ref[i * rows : (i + 1) * rows, :] = (wide * inv_rms).astype(bf16)

    gathered = dot(p_ref[...], normed_ref[...]).astype(bf16)
    out_ref[...] = to_wire(permutation(True), gathered, features // CHUNKS)


def pack_grad_kernel(p_ref, gate_ref, own_ref, partner_ref, out_ref):
    rows, features = own_ref.shape
    p = p_ref[...]
    gathered = dot(p[:, :rows], own_ref[...]) + dot(p[:, rows:], partner_ref[...])
    scaled = (gathered * gate_ref[...]).astype(bf16)
    out_ref[...] = to_wire(permutation(True), scaled, features // CHUNKS)


def pack(kernel, slots, rows, features, scratch, specs, args):
    wire = BLOCK * CHUNKS
    return pl.pallas_call(
        kernel,
        grid=(slots // BLOCK,),
        in_specs=specs,
        out_specs=pl.BlockSpec((wire, features // CHUNKS), lambda i: (i, 0)),
        out_shape=jax.ShapeDtypeStruct((slots * CHUNKS, features // CHUNKS), bf16),
        scratch_shapes=scratch,
        compiler_params=pltpu.CompilerParams(vmem_limit_bytes=VMEM_LIMIT),
        cost_estimate=pl.CostEstimate(
            flops=2 * slots * (2 * rows + wire) * features,
            bytes_accessed=2 * (2 * rows + slots) * features,
            transcendentals=0,
        ),
    )(*args)


def from_wire(wire_ref, out_ref):
    size, width = BLOCK * CHUNKS, wire_ref.shape[1]
    perm = permutation(False)

    def block(i, carry):
        turned = dot(perm, wire_ref[pl.ds(pl.multiple_of(i * size, size), size), :]).astype(bf16)
        at = pl.ds(pl.multiple_of(i * BLOCK, BLOCK), BLOCK)
        for c in range(CHUNKS):
            out_ref[at, c * width : (c + 1) * width] = turned[c * BLOCK : (c + 1) * BLOCK]
        return carry

    lax.fori_loop(0, out_ref.shape[0] // BLOCK, block, 0)


def put_on_wire(rows_ref, out_ref):
    size, width = BLOCK * CHUNKS, out_ref.shape[1]
    perm = permutation(True)

    def block(i, carry):
        at = pl.ds(pl.multiple_of(i * BLOCK, BLOCK), BLOCK)
        out_ref[pl.ds(pl.multiple_of(i * size, size), size), :] = to_wire(perm, rows_ref[at, :], width)
        return carry

    lax.fori_loop(0, rows_ref.shape[0] // BLOCK, block, 0)


def forward_kernel(wire_ref, gate_ref, up_ref, down_ref, out_ref, a_ref, b_ref, x_ref, product_ref):
    step = pl.program_id(0)
    tiles = product_ref.shape[0]
    width = out_ref.shape[1]

    @pl.when(step == 0)
    def _():
        from_wire(wire_ref, x_ref)

    @pl.when(step < tiles)
    def _():
        hidden_a = dot(x_ref[...], gate_ref[...])
        hidden_b = dot(x_ref[...], up_ref[...])
        a_ref[...] = hidden_a
        b_ref[...] = hidden_b
        product_ref[step] = (hidden_a * jax.nn.sigmoid(hidden_a) * hidden_b).astype(bf16)

    for c in range(CHUNKS):
        @pl.when(step == tiles + c)
        def _():
            product = jnp.concatenate([product_ref[n] for n in range(tiles)], axis=1)
            x_ref[:, c * width : (c + 1) * width] = dot(product, down_ref[...]).astype(bf16)

    @pl.when(step == tiles + CHUNKS - 1)
    def _():
        put_on_wire(x_ref, out_ref)


def backward_kernel(wire_ref, a_ref, b_ref, down_ref, gate_ref, up_ref, out_ref, x_ref, grad_ref):
    step = pl.program_id(0)
    tiles = grad_ref.shape[0] // 2
    width = out_ref.shape[1]

    @pl.when(step == 0)
    def _():
        from_wire(wire_ref, x_ref)

    @pl.when(step < tiles)
    def _():
        grad_act = dot_nt(x_ref[...], down_ref[...])
        hidden_a, hidden_b = a_ref[...], b_ref[...]
        sigmoid_a = jax.nn.sigmoid(hidden_a)
        slope = sigmoid_a * (1.0 + hidden_a * (1.0 - sigmoid_a))
        grad_ref[step] = (grad_act * hidden_b * slope).astype(bf16)
        grad_ref[tiles + step] = (grad_act * (hidden_a * sigmoid_a)).astype(bf16)

    for c in range(CHUNKS):
        @pl.when(step == tiles + c)
        def _():
            grad_a = jnp.concatenate([grad_ref[n] for n in range(tiles)], axis=1)
            grad_b = jnp.concatenate([grad_ref[tiles + n] for n in range(tiles)], axis=1)
            rows = dot_nt(grad_a, gate_ref[...]) + dot_nt(grad_b, up_ref[...])
            x_ref[:, c * width : (c + 1) * width] = rows.astype(bf16)

    @pl.when(step == tiles + CHUNKS - 1)
    def _():
        put_on_wire(x_ref, out_ref)


def expert_call(kernel, wire, weights, hidden, slots, features, units):
    tile = 256
    tiles = units // tile
    width = features // CHUNKS

    def early(i):
        return jnp.minimum(i, tiles - 1)

    def late(i):
        return jnp.maximum(i - tiles, 0)

    whole = pl.BlockSpec((slots * CHUNKS, width), lambda i: (0, 0))
    hidden_spec = pl.BlockSpec((slots, tile), lambda i: (0, early(i)))
    wire_shape = jax.ShapeDtypeStruct((slots * CHUNKS, width), bf16)
    if hidden is None:
        in_specs = [
            whole,
            pl.BlockSpec((features, tile), lambda i: (0, early(i))),
            pl.BlockSpec((features, tile), lambda i: (0, early(i))),
            pl.BlockSpec((units, width), lambda i: (0, late(i))),
        ]
        out_specs = [whole, hidden_spec, hidden_spec]
        out_shape = [wire_shape] + [jax.ShapeDtypeStruct((slots, units), f32)] * 2
        scratch = [pltpu.VMEM((slots, features), bf16), pltpu.VMEM((tiles, slots, tile), bf16)]
        args = (wire, *weights)
    else:
        in_specs = [
            whole,
            hidden_spec,
            hidden_spec,
            pl.BlockSpec((tile, features), lambda i: (early(i), 0)),
            pl.BlockSpec((width, units), lambda i: (late(i), 0)),
            pl.BlockSpec((width, units), lambda i: (late(i), 0)),
        ]
        out_specs, out_shape = whole, wire_shape
        scratch = [pltpu.VMEM((slots, features), bf16), pltpu.VMEM((2 * tiles, slots, tile), bf16)]
        args = (wire, *hidden, *weights)
    return pl.pallas_call(
        kernel,
        grid=(tiles + CHUNKS,),
        in_specs=in_specs,
        out_specs=out_specs,
        out_shape=out_shape,
        scratch_shapes=scratch,
        compiler_params=pltpu.CompilerParams(vmem_limit_bytes=VMEM_LIMIT),
        cost_estimate=pl.CostEstimate(
            flops=8 * slots * units * features,
            bytes_accessed=6 * units * features + 4 * slots * features + 8 * slots * units,
            transcendentals=slots * units,
        ),
    )(*args)


def combine_kernel(wire_ref, *refs):
    *matrix_refs, own_ref, partner_ref, rows_ref = refs
    step = pl.program_id(0)
    width = wire_ref.shape[1]
    turned = dot(permutation(False), wire_ref[...]).astype(bf16)
    at = pl.ds(pl.multiple_of(step * BLOCK, BLOCK), BLOCK)
    for c in range(CHUNKS):
        rows_ref[at, c * width : (c + 1) * width] = turned[c * BLOCK : (c + 1) * BLOCK]

    @pl.when(step == pl.num_programs(0) - 1)
    def _():
        count = own_ref.shape[0]
        rows = rows_ref[...]
        total = dot(matrix_refs[0][...], rows)
        for ref in matrix_refs[1:]:
            total = total + dot(ref[...], rows)
        own_ref[...] = total[:count].astype(own_ref.dtype)
        partner_ref[...] = total[count:].astype(partner_ref.dtype)


def combine(wire, matrices, slots, rows, features):
    size = BLOCK * CHUNKS
    matrix_spec = pl.BlockSpec((2 * rows, slots), lambda i: (0, 0))
    part_spec = pl.BlockSpec((rows, features), lambda i: (0, 0))
    return pl.pallas_call(
        combine_kernel,
        grid=(slots // BLOCK,),
        in_specs=[pl.BlockSpec((size, features // CHUNKS), lambda i: (i, 0))] + [matrix_spec] * len(matrices),
        out_specs=[part_spec, part_spec],
        out_shape=[jax.ShapeDtypeStruct((rows, features), f32)] * 2,
        scratch_shapes=[pltpu.VMEM((slots, features), bf16)],
        compiler_params=pltpu.CompilerParams(vmem_limit_bytes=VMEM_LIMIT),
        cost_estimate=pl.CostEstimate(
            flops=2 * slots * (2 * rows * len(matrices) + size) * features,
            bytes_accessed=2 * slots * features + 16 * rows * features,
            transcendentals=0,
        ),
    )(wire, *matrices)


def local(tokens, grad_out, routes, gates, gate_weight, up_weight, down_weight):
    rows, features = tokens.shape
    top = routes.shape[1]
    units = gate_weight.shape[2]
    chips = lax.axis_size("dev")
    cap = rows * top * 5 // (4 * chips * lax.axis_size("role"))
    per_chip = 2 * cap
    slots = chips * per_chip
    role = lax.axis_index("role").astype(jnp.int32).reshape(1)
    swap = [(0, 1), (1, 0)]

    def other(array):
        return lax.ppermute(array, "role", swap)

    route_info = jnp.concatenate([routes.astype(f32), gates], axis=1).T
    route_other = other(route_info)
    tokens_other = other(tokens)
    grad_other = other(grad_out)

    place = np.arange(slots)
    expand = (place[:, None] // per_chip == np.arange(chips)[None, :]).astype(np.float32)
    source, number = place % per_chip // cap, place % cap
    target = np.where(np.arange(2 * rows)[None, :] // rows == source[:, None], number[:, None] + 1, -1)
    vmem = pl.BlockSpec(memory_space=pltpu.VMEM)
    p, p_turned, slot_gate, gate_hi, gate_lo = pl.pallas_call(
        route_kernel,
        in_specs=[pl.BlockSpec(memory_space=pltpu.SMEM)] + [vmem] * 4,
        out_specs=[vmem] * 5,
        out_shape=[
            jax.ShapeDtypeStruct((slots, 2 * rows), bf16),
            jax.ShapeDtypeStruct((2 * rows, slots), bf16),
            jax.ShapeDtypeStruct((slots, 1), f32),
            jax.ShapeDtypeStruct((2 * rows, slots), bf16),
            jax.ShapeDtypeStruct((2 * rows, slots), bf16),
        ],
    )(role, route_info, route_other, jnp.asarray(expand, bf16), jnp.asarray(target, bf16))

    p_spec = pl.BlockSpec((BLOCK, 2 * rows), lambda i: (i, 0))
    slot_spec = pl.BlockSpec((BLOCK, 1), lambda i: (i, 0))
    rows_spec = pl.BlockSpec((rows, features), lambda i: (0, 0))
    normed_wire = pack(
        pack_normed_kernel, slots, rows, features, [pltpu.VMEM((2 * rows, features), bf16)],
        [p_spec, rows_spec, rows_spec], (p, tokens, tokens_other),
    )
    grad_wire = pack(
        pack_grad_kernel, slots, rows, features, [],
        [p_spec, slot_spec, rows_spec, rows_spec], (p, slot_gate, grad_out, grad_other),
    )

    def exchange(wire):
        parts = wire.reshape(chips, per_chip * CHUNKS, features // CHUNKS)
        parts = lax.all_to_all(parts, "dev", split_axis=0, concat_axis=0, tiled=True)
        return parts.reshape(wire.shape)

    gate_local, up_local, down_local = gate_weight[0], up_weight[0], down_weight[0]
    normed_in = exchange(normed_wire)
    grad_in_wire = exchange(grad_wire)
    out_wire, hidden_a, hidden_b = expert_call(
        forward_kernel, normed_in, (gate_local, up_local, down_local), None, slots, features, units
    )
    out_back = exchange(out_wire)
    rows_wire = expert_call(
        backward_kernel, grad_in_wire, (down_local, gate_local, up_local), (hidden_a, hidden_b), slots, features, units
    )
    rows_back = exchange(rows_wire)

    out_own, out_partner = combine(out_back, (gate_hi, gate_lo), slots, rows, features)
    tokens_wide = tokens.astype(f32)
    layer_out = (tokens_wide + (out_own + other(out_partner))).astype(bf16)

    grad_own, grad_partner = combine(rows_back, (p_turned,), slots, rows, features)
    grad_normed = grad_own + other(grad_partner)
    inv_rms = lax.rsqrt(jnp.mean(tokens_wide * tokens_wide, axis=1, keepdims=True) + epsilon)
    projected = jnp.mean(grad_normed * tokens_wide, axis=1, keepdims=True)
    grad_in = grad_out.astype(f32) + inv_rms * grad_normed - tokens_wide * inv_rms**3 * projected
    return (layer_out, grad_in.astype(bf16))


def solution(mesh):
    split = P(("role", "dev"), None)
    split_weight = P(("role", "dev"), None, None)
    in_specs = (split, split, split, split, split_weight, split_weight, split_weight)
    return jax.shard_map(local, mesh=mesh, in_specs=in_specs, out_specs=(split, split), check_vma=False)
```

time: 628 us -> 348 us (0.55)
  the two profiles are of different devices: /device:TPU:13 before, /device:TPU:1 now
where the time goes in v1:
time: 348 us; the launch traced here: 342 us
  waiting for transfers between devices  115 us (33%)
  Pallas kernels  108 us (31%)
  blocking collectives  65.4 us (19%)
  starting transfers between devices  45.1 us (13%)
  other arithmetic  5.57 us (2%)
    all_to_all x3, waiting for transfers between devices, exchange(): lax.all_to_all(parts, 'dev', split_axis=0, concat_axis=0, tiled=True)  110 us
    all_to_all x1, blocking collectives, exchange(): lax.all_to_all(parts, 'dev', split_axis=0, concat_axis=0, tiled=True)  65.4 us
    pallas_call x2, Pallas kernels, expert_call(): pl.pallas_call(kernel, grid=(tiles + CHUNKS,), in_specs=in_specs, out_spe...  62.1 us
    all_to_all x3, starting transfers between devices, exchange(): lax.all_to_all(parts, 'dev', split_axis=0, concat_axis=0, tiled=True)  37.3 us
    pallas_call x2, Pallas kernels, combine(): pl.pallas_call(combine_kernel, grid=(slots // BLOCK,), in_specs=[pl.Block...  22.8 us
    pallas_call x2, Pallas kernels, pack(): pl.pallas_call(kernel, grid=(slots // BLOCK,), in_specs=specs, out_specs=...  20.3 us
    ppermute x5, starting transfers between devices, other(): return lax.ppermute(array, 'role', swap)  7.79 us
  transfers between devices with their start and end apart: 8, of which 6 were waited for; matrix products, arithmetic and copies ran while one was open for 1% of the time, Pallas kernels for 19%

profile of v1, /device:TPU:1, one launch (start us, length us, event | category | flops | bytes accessed | tf_op | source)
XLA Modules:
  0.0 342.0 jit_solution(9652765562628622574)
XLA Ops:
  0.6 1.5 collective-permute-start.1
  2.1 0.7 convert_element_type.16
  2.8 0.7 maximum_bitcast_fusion.own_ref
  3.5 0.0 collective-permute-start
  3.5 1.1 collective-permute-done.partner_ref
  4.7 0.6 copy-done.6
  5.3 2.9 shard_map.104
  8.2 0.0 collective-permute-done.1.partner_ref
  8.2 0.9 copy-done.7
  9.1 10.5 %shard_map.105 = bf16[2560,896]{1,0:T(8,128)(2,1)} custom-call(bf16[640,256]{1,0:T(8,128)(2,1)} %get-tuple-element.14.p_ref, bf16[128,3584]{1,0:T(8,128)(2,1)} %own_ref.2, bf16[128,3584]{1,0:T(8,128)(2,1)} %copy-done.7), custom_call_target="tpu_custom_call" | custom-call | flops 2348810240 | bytes 6422528 | tf_op jit(solution)/shard_map/pallas_call | solution.py:99
  19.6 11.6 %all-to-all-start = ((bf16[64,40,896]{2,1,0:T(8,128)(2,1)}), bf16[64,40,896]{2,1,0:T(8,128)(2,1)}, u32[]{:S(2)}, u32[]{:S(2)}) async-start(bf16[64,40,896]{2,1,0:T(8,128)(2,1)} %bitcast.16), calls=%async_computation | async-start | bytes 9175040 | tf_op jit(solution)/shard_map/all_to_all | solution.py:344
  31.2 0.5 collective-permute-start.3
  31.8 2.1 collective-permute-done.3.partner_ref
  33.9 0.9 copy-done.8
  34.8 9.8 %shard_map.108 = bf16[2560,896]{1,0:T(8,128)(2,1)} custom-call(bf16[640,256]{1,0:T(8,128)(2,1)} %get-tuple-element.14.p_ref, f32[640,1]{1,0:T(8,128)} %get-tuple-element.20.gate_ref, bf16[128,3584]{1,0:T(8,128)(2,1)} %own_ref.3, bf16[128,3584]{1,0:T(8,128)(2,1)} %copy-done.8), custom_call_target="tpu_custom_call" | custom-call | flops 2348810240 | bytes 6422528 | tf_op jit(solution)/shard_map/pallas_call | solution.py:99
  44.6 43.5 %all-to-all-done = bf16[64,40,896]{2,1,0:T(8,128)(2,1)} async-done(((bf16[64,40,896]{2,1,0:T(8,128)(2,1)}), bf16[64,40,896]{2,1,0:T(8,128)(2,1)}, u32[]{:S(2)}, u32[]{:S(2)}) %all-to-all-start) | async-done | bytes 4587552 | tf_op jit(solution)/shard_map/all_to_all | solution.py:344
  88.0 16.4 %all-to-all-start.2 = ((bf16[64,40,896]{2,1,0:T(8,128)(2,1)}), bf16[64,40,896]{2,1,0:T(8,128)(2,1)}, u32[]{:S(2)}, u32[]{:S(2)}) async-start(bf16[64,40,896]{2,1,0:T(8,128)(2,1)} %bitcast.15), calls=%async_computation.2 | async-start | bytes 9175040 | tf_op jit(solution)/shard_map/all_to_all | solution.py:344
  104.5 30.6 %shard_map.106 = (bf16[2560,896]{1,0:T(8,128)(2,1)}, f32[640,1024]{1,0:T(8,128)}, f32[640,1024]{1,0:T(8,128)}) custom-call(bf16[2560,896]{1,0:T(8,128)(2,1)} %bitcast.3.wire_ref, bf16[3584,1024]{1,0:T(8,128)(2,1)} %bitcast.19, bf16[3584,1024]{1,0:T(8,128)(2,1)} %bitcast.21, bf16[1024,3584]{1,0:T(8,128)(2,1)} %bitcast.23), custom_call_target="tpu_custom_call" | custom-call | flops 18790481920 | bytes 36438016 | tf_op jit(solution)/shard_map/pallas_call | solution.py:237
  135.1 24.7 %all-to-all-done.2 = bf16[64,40,896]{2,1,0:T(8,128)(2,1)} async-done(((bf16[64,40,896]{2,1,0:T(8,128)(2,1)}), bf16[64,40,896]{2,1,0:T(8,128)(2,1)}, u32[]{:S(2)}, u32[]{:S(2)}) %all-to-all-start.2) | async-done | bytes 4587552 | tf_op jit(solution)/shard_map/all_to_all | solution.py:344
  159.8 31.5 %shard_map.109 = bf16[2560,896]{1,0:T(8,128)(2,1)} custom-call(bf16[2560,896]{1,0:T(8,128)(2,1)} %bitcast.10.wire_ref, f32[640,1024]{1,0:T(8,128)} %get-tuple-element.21.a_ref, f32[640,1024]{1,0:T(8,128)} %get-tuple-element.22.b_ref, bf16[1024,3584]{1,0:T(8,128)(2,1)} %bitcast.24, bf16[3584,1024]{1,0:T(8,128)(2,1)} %bitcast.20, bf16[3584,1024]{1,0:T(8,128)(2,1)} %bitcast.22), custom_call_target="tpu_custom_call" | custom-call | flops 18790481920 | bytes 36438016 | tf_op jit(solution)/shard_map/pallas_call | solution.py:237
  191.3 65.4 %all_to_all.20 = bf16[64,40,896]{2,1,0:T(8,128)(2,1)} all-to-all(bf16[64,40,896]{2,1,0:T(8,128)(2,1)} %bitcast.18), channel_id=1, replica_groups=mesh['role'=2,'dev'=64] {'dev'}, dimensions={0} | all-to-all | bytes 9175040 | tf_op jit(solution)/shard_map/all_to_all | solution.py:344
  256.7 9.3 %all-to-all-start.1 = ((bf16[64,40,896]{2,1,0:T(8,128)(2,1)}), bf16[64,40,896]{2,1,0:T(8,128)(2,1)}, u32[]{:S(2)}, u32[]{:S(2)}) async-start(bf16[64,40,896]{2,1,0:T(8,128)(2,1)} %bitcast.14), calls=%async_computation.1 | async-start | bytes 9175040 | tf_op jit(solution)/shard_map/all_to_all | solution.py:344
  265.9 10.6 %shard_map.110 = (f32[128,3584]{1,0:T(8,128)}, f32[128,3584]{1,0:T(8,128)}) custom-call(bf16[2560,896]{1,0:T(8,128)(2,1)} %bitcast.17, bf16[256,640]{1,0:T(8,128)(2,1)} %get-tuple-element.23.refs_0_), custom_call_target="tpu_custom_call" | custom-call | flops 2348810240 | bytes 11927552 | tf_op jit(solution)/shard_map/pallas_call | solution.py:277
  276.5 1.5 collective-permute-start.4
  278.0 41.5 %all-to-all-done.1 = bf16[64,40,896]{2,1,0:T(8,128)(2,1)} async-done(((bf16[64,40,896]{2,1,0:T(8,128)(2,1)}), bf16[64,40,896]{2,1,0:T(8,128)(2,1)}, u32[]{:S(2)}, u32[]{:S(2)}) %all-to-all-start.1) | async-done | bytes 4587552 | tf_op jit(solution)/shard_map/all_to_all | solution.py:344
  319.5 12.2 %shard_map.107 = (f32[128,3584]{1,0:T(8,128)}, f32[128,3584]{1,0:T(8,128)}) custom-call(bf16[2560,896]{1,0:T(8,128)(2,1)} %bitcast.8.wire_ref, bf16[256,640]{1,0:T(8,128)(2,1)} %get-tuple-element.16.refs_0_, bf16[256,640]{1,0:T(8,128)(2,1)} %get-tuple-element.17.refs_1_), custom_call_target="tpu_custom_call" | custom-call | flops 3523215360 | bytes 11927552 | tf_op jit(solution)/shard_map/pallas_call | solution.py:277
  331.7 4.3 %collective-permute-start.2 = (f32[128,3584]{1,0:T(8,128)}, f32[128,3584]{1,0:T(8,128)S(1)}, u32[]{:S(2)}, u32[]{:S(2)}) collective-permute-start(f32[128,3584]{1,0:T(8,128)} %get-tuple-element.19), channel_id=1, source_target_pairs={{0,64},{64,0},{1,65},{65,1},{2,66},{66,2},{3,67},{67,3},{4,68},{68... | collective-permute-start | bytes 5505032 | tf_op jit(solution)/shard_map/ppermute | solution.py:305
  336.0 0.0 collective-permute-done.4
  336.0 0.0 copy-start.4
  336.0 1.8 fusion.1
  337.8 1.8 collective-permute-done.2
  339.6 2.4 fusion.4
  (16 shorter events, 0.0 us)
Async XLA Ops:
  0.6 7.6 %collective-permute-start.1 = (bf16[128,3584]{1,0:T(8,128)(2,1)}, bf16[128,3584]{1,0:T(8,128)(2,1)S(1)}, u32[]{:S(2)}, u32[]{:S(2)}) collective-permute-start(bf16[128,3584]{1,0:T(8,128)(2,1)} %own_ref.2), channel_id=1, source_target_pairs={{0,64},{64,0},{1,65},{65,1},{2,66},{66,2},{3,67},{67,3},{4,68},{68... | collective-permute-start | bytes 2752520 | tf_op jit(solution)/shard_map/ppermute | solution.py:305
  3.5 1.2 copy-start.5
  3.5 1.2 collective-permute-start
  4.7 0.6 copy-start.6
  8.2 0.9 copy-start.7
  19.6 11.6 %copy-start.3 = (bf16[128,3584]{1,0:T(8,128)(2,1)S(1)}, bf16[128,3584]{1,0:T(8,128)(2,1)}, u32[]{:S(2)}) copy-start(bf16[128,3584]{1,0:T(8,128)(2,1)} %own_ref.3) | copy-start | bytes 2752516
  19.6 68.4 %all-to-all-start = ((bf16[64,40,896]{2,1,0:T(8,128)(2,1)}), bf16[64,40,896]{2,1,0:T(8,128)(2,1)}, u32[]{:S(2)}, u32[]{:S(2)}) async-start(bf16[64,40,896]{2,1,0:T(8,128)(2,1)} %bitcast.16), calls=%async_computation | async-start | bytes 9175040 | tf_op jit(solution)/shard_map/all_to_all | solution.py:344
  31.2 2.6 collective-permute-start.3
  33.9 0.9 copy-start.8
  88.0 71.8 %all-to-all-start.2 = ((bf16[64,40,896]{2,1,0:T(8,128)(2,1)}), bf16[64,40,896]{2,1,0:T(8,128)(2,1)}, u32[]{:S(2)}, u32[]{:S(2)}) async-start(bf16[64,40,896]{2,1,0:T(8,128)(2,1)} %bitcast.15), calls=%async_computation.2 | async-start | bytes 9175040 | tf_op jit(solution)/shard_map/all_to_all | solution.py:344
  256.7 62.8 %all-to-all-start.1 = ((bf16[64,40,896]{2,1,0:T(8,128)(2,1)}), bf16[64,40,896]{2,1,0:T(8,128)(2,1)}, u32[]{:S(2)}, u32[]{:S(2)}) async-start(bf16[64,40,896]{2,1,0:T(8,128)(2,1)} %bitcast.14), calls=%async_computation.1 | async-start | bytes 9175040 | tf_op jit(solution)/shard_map/all_to_all | solution.py:344
  276.5 59.5 %collective-permute-start.4 = (f32[128,3584]{1,0:T(8,128)}, f32[128,3584]{1,0:T(8,128)S(1)}, u32[]{:S(2)}, u32[]{:S(2)}) collective-permute-start(f32[128,3584]{1,0:T(8,128)} %get-tuple-element.25), channel_id=1, source_target_pairs={{0,64},{64,0},{1,65},{65,1},{2,66},{66,2},{3,67},{67,3},{4,68},{68... | collective-permute-start | bytes 5505032 | tf_op jit(solution)/shard_map/ppermute | solution.py:305
  319.5 16.5 %copy-start = (f32[128,3584]{1,0:T(8,128)S(1)}, f32[128,3584]{1,0:T(8,128)}, u32[]{:S(2)}) copy-start(f32[128,3584]{1,0:T(8,128)} %get-tuple-element.24) | copy-start | bytes 5505028
  331.7 7.9 %collective-permute-start.2 = (f32[128,3584]{1,0:T(8,128)}, f32[128,3584]{1,0:T(8,128)S(1)}, u32[]{:S(2)}, u32[]{:S(2)}) collective-permute-start(f32[128,3584]{1,0:T(8,128)} %get-tuple-element.19), channel_id=1, source_target_pairs={{0,64},{64,0},{1,65},{65,1},{2,66},{66,2},{3,67},{67,3},{4,68},{68... | collective-permute-start | bytes 5505032 | tf_op jit(solution)/shard_map/ppermute | solution.py:305
  336.0 3.6 %copy-start.1 = (bf16[128,3584]{1,0:T(8,128)(2,1)S(1)}, bf16[128,3584]{1,0:T(8,128)(2,1)}, u32[]{:S(2)}) copy-start(bf16[128,3584]{1,0:T(8,128)(2,1)} %own_ref.2) | copy-start | bytes 2752516
  336.0 3.6 %copy-start.2 = (f32[128,3584]{1,0:T(8,128)S(1)}, f32[128,3584]{1,0:T(8,128)}, u32[]{:S(2)}) copy-start(f32[128,3584]{1,0:T(8,128)} %get-tuple-element.18) | copy-start | bytes 5505028
  336.0 3.6 %copy-start.4 = (bf16[128,3584]{1,0:T(8,128)(2,1)S(1)}, bf16[128,3584]{1,0:T(8,128)(2,1)}, u32[]{:S(2)}) copy-start(bf16[128,3584]{1,0:T(8,128)(2,1)} %own_ref.3) | copy-start | bytes 2752516

commit v2 on v1

--- a/solution.py
+++ b/solution.py
@@ -1,6 +1,7 @@
+import functools
+
 import jax
 import jax.numpy as jnp
-import numpy as np
 from jax import lax
 from jax.experimental import pallas as pl
 from jax.experimental.pallas import tpu as pltpu
@@ -10,7 +11,9 @@
 bf16, f32 = jnp.bfloat16, jnp.float32
 CHUNKS = 4
 BLOCK = 64
+PACK = 320
 VMEM_LIMIT = 60 * 1024 * 1024
+SMALL_LIMIT = 40 * 1024 * 1024
 
 
 def dot(a, b):
@@ -33,83 +36,131 @@
     return dot(perm, stacked).astype(bf16)
 
 
-def route_kernel(role_ref, own_ref, partner_ref, expand_ref, target_ref, p_ref, pt_ref, gate_ref, hi_ref, lo_ref):
-    experts = expand_ref.shape[1]
-    rows = own_ref.shape[1]
-    named = lax.broadcasted_iota(jnp.int32, (experts, rows), 0) + role_ref[0] * experts
-    named = named.astype(f32)
+def slot_tables(chips, slots, rows):
+    per_chip = slots // chips
+    cap = per_chip // 2
+    slot = lax.broadcasted_iota(jnp.int32, (slots, chips), 0)
+    first = lax.broadcasted_iota(jnp.int32, (slots, chips), 1) * per_chip
+    expand = jnp.where((slot >= first) & (slot < first + per_chip), 1.0, 0.0)
+    place = slot[:, :1].astype(f32) - jnp.sum(jnp.where(expand > 0.0, first.astype(f32), 0.0), axis=1, keepdims=True)
+    partner = place >= cap
+    rank = jnp.where(partner, place - cap, place) + 1.0
+    lane = lax.broadcasted_iota(jnp.int32, (slots, 2 * rows), 1).astype(f32)
+    side = jnp.where(partner, 1.0, 0.0)
+    target = jnp.where(jnp.where(lane >= rows, 1.0, 0.0) == side, rank, -1.0)
+    return expand.astype(bf16), target
+
+
+def chosen_slots(role, sides, chips, slots):
+    top, rows = sides[0][0].shape
+    expand, target = slot_tables(chips, slots, rows)
+    named = lax.broadcasted_iota(jnp.int32, (chips, rows), 0) + role * chips
     before = lax.broadcasted_iota(jnp.int32, (rows, rows), 0)
     after = lax.broadcasted_iota(jnp.int32, (rows, rows), 1)
     strict = jnp.where(before < after, 1.0, 0.0).astype(bf16)
     ranks, gates = [], []
-    for ref in (own_ref, partner_ref):
-        top = ref.shape[0] // 2
-        uses = jnp.zeros((experts, rows), f32)
-        gate = jnp.zeros((experts, rows), f32)
+    for route_ref, gate_ref in sides:
+        uses = jnp.zeros((chips, rows), f32)
+        gate = jnp.zeros((chips, rows), f32)
         for k in range(top):
-            hit = named == ref[k : k + 1, :]
+            hit = named == route_ref[k : k + 1, :]
             uses = jnp.where(hit, 1.0, uses)
-            gate = jnp.where(hit, ref[top + k : top + k + 1, :], gate)
+            gate = jnp.where(hit, gate_ref[k : k + 1, :], gate)
         ranks.append(uses * (dot(uses.astype(bf16), strict) + 1.0))
         gates.append(gate)
-    expand = expand_ref[...]
     rank = jnp.concatenate(ranks, axis=1).astype(bf16)
     gate = jnp.concatenate(gates, axis=1)
-    chosen = dot(expand, rank) == target_ref[...].astype(f32)
+    chosen = dot(expand, rank) == target
     first = gate.astype(bf16)
     rest = gate - first.astype(f32)
     second = rest.astype(bf16)
     third = (rest - second.astype(f32)).astype(bf16)
     spread = dot(expand, first) + (dot(expand, second) + dot(expand, third))
-    spread = jnp.where(chosen, spread, 0.0)
-    one_hot = jnp.where(chosen, 1.0, 0.0)
-    p_ref[...] = one_hot.astype(bf16)
-    pt_ref[...] = jnp.transpose(one_hot).astype(bf16)
-    gate_ref[...] = jnp.sum(spread, axis=1, keepdims=True)
-    turned = jnp.transpose(spread)
-    hi = turned.astype(bf16)
-    hi_ref[...] = hi
-    lo_ref[...] = (turned - hi.astype(f32)).astype(bf16)
-
-
-def pack_normed_kernel(p_ref, own_ref, partner_ref, out_ref, normed_ref):
-    rows, features = own_ref.shape
-
-    @pl.when(pl.program_id(0) == 0)
-    def _():
-        for i, ref in enumerate((own_ref, partner_ref)):
+    return jnp.where(chosen, 1.0, 0.0), jnp.where(chosen, spread, 0.0)
+
+
+def wire_blocks(out_ref, perm, rows):
+    size, width = BLOCK * CHUNKS, out_ref.shape[1]
+    for i in range(rows.shape[0] // BLOCK):
+        out_ref[i * size : (i + 1) * size, :] = to_wire(perm, rows[i * BLOCK : (i + 1) * BLOCK], width)
+
+
+def pack_kernel(
+    chips, role_ref, route_ref, route_other_ref, gate_ref, gate_other_ref,
+    tokens_ref, tokens_other_ref, grad_ref, grad_other_ref,
+    normed_wire_ref, grad_wire_ref, pt_ref, hi_ref, lo_ref,
+    normed_ref, p_ref, slot_gate_ref, perm_ref,
+):
+    rows = tokens_ref.shape[0]
+    slots = p_ref.shape[0]
+    step = pl.program_id(0)
+    half = slots // PACK
+
+    @pl.when(step == 0)
+    def _():
+        perm_ref[...] = permutation(True)
+        sides = ((route_ref, gate_ref), (route_other_ref, gate_other_ref))
+        one_hot, spread = chosen_slots(role_ref[0], sides, chips, slots)
+        p_ref[...] = one_hot.astype(bf16)
+        slot_gate_ref[...] = jnp.sum(spread, axis=1, keepdims=True)
+        pt_ref[...] = jnp.transpose(one_hot).astype(bf16)
+        turned = jnp.transpose(spread)
+        hi = turned.astype(bf16)
+        hi_ref[...] = hi
+        lo_ref[...] = (turned - hi.astype(f32)).astype(bf16)
+        for i, ref in enumerate((tokens_ref, tokens_other_ref)):
             wide = ref[...].astype(f32)
             inv_rms = lax.rsqrt(jnp.mean(wide * wide, axis=1, keepdims=True) + epsilon)
             normed_ref[i * rows : (i + 1) * rows, :] = (wide * inv_rms).astype(bf16)
 
-    gathered = dot(p_ref[...], normed_ref[...]).astype(bf16)
-    out_ref[...] = to_wire(permutation(True), gathered, features // CHUNKS)
-
-
-def pack_grad_kernel(p_ref, gate_ref, own_ref, partner_ref, out_ref):
-    rows, features = own_ref.shape
-    p = p_ref[...]
-    gathered = dot(p[:, :rows], own_ref[...]) + dot(p[:, rows:], partner_ref[...])
-    scaled = (gathered * gate_ref[...]).astype(bf16)
-    out_ref[...] = to_wire(permutation(True), scaled, features // CHUNKS)
-
-
-def pack(kernel, slots, rows, features, scratch, specs, args):
-    wire = BLOCK * CHUNKS
+    at = pl.ds(pl.multiple_of(lax.rem(step, half) * PACK, PACK), PACK)
+
+    @pl.when(step < half)
+    def _():
+        wire_blocks(normed_wire_ref, perm_ref[...], dot(p_ref[at, :], normed_ref[...]).astype(bf16))
+
+    @pl.when(step >= half)
+    def _():
+        p = p_ref[at, :]
+        gathered = dot(p[:, :rows], grad_ref[...]) + dot(p[:, rows:], grad_other_ref[...])
+        wire_blocks(grad_wire_ref, perm_ref[...], (gathered * slot_gate_ref[at, :]).astype(bf16))
+
+
+def pack(role, routes, gates, tokens, grads, chips, slots):
+    rows, features = tokens[0].shape
+    top = routes[0].shape[0]
+    half = slots // PACK
+    width = features // CHUNKS
+
+    def fixed(*shape):
+        return pl.BlockSpec(shape, lambda i: (0,) * len(shape))
+
+    lane_spec, rows_spec, turned_spec = fixed(top, rows), fixed(rows, features), fixed(2 * rows, slots)
+    wire_shape = jax.ShapeDtypeStruct((slots * CHUNKS, width), bf16)
+    turned_shape = jax.ShapeDtypeStruct((2 * rows, slots), bf16)
     return pl.pallas_call(
-        kernel,
-        grid=(slots // BLOCK,),
-        in_specs=specs,
-        out_specs=pl.BlockSpec((wire, features // CHUNKS), lambda i: (i, 0)),
-        out_shape=jax.ShapeDtypeStruct((slots * CHUNKS, features // CHUNKS), bf16),
-        scratch_shapes=scratch,
+        functools.partial(pack_kernel, chips),
+        grid=(2 * half,),
+        in_specs=[pl.BlockSpec(memory_space=pltpu.SMEM)] + [lane_spec] * 4 + [rows_spec] * 4,
+        out_specs=[
+            pl.BlockSpec((PACK * CHUNKS, width), lambda i: (jnp.minimum(i, half - 1), 0)),
+            pl.BlockSpec((PACK * CHUNKS, width), lambda i: (jnp.maximum(i - half, 0), 0)),
+            turned_spec, turned_spec, turned_spec,
+        ],
+        out_shape=[wire_shape, wire_shape, turned_shape, turned_shape, turned_shape],
+        scratch_shapes=[
+            pltpu.VMEM((2 * rows, features), bf16),
+            pltpu.VMEM((slots, 2 * rows), bf16),
+            pltpu.VMEM((slots, 1), f32),
+            pltpu.VMEM((BLOCK * CHUNKS, BLOCK * CHUNKS), bf16),
+        ],
         compiler_params=pltpu.CompilerParams(vmem_limit_bytes=VMEM_LIMIT),
         cost_estimate=pl.CostEstimate(
-            flops=2 * slots * (2 * rows + wire) * features,
-            bytes_accessed=2 * (2 * rows + slots) * features,
+            flops=4 * slots * (2 * rows + BLOCK * CHUNKS) * features,
+            bytes_accessed=4 * (2 * rows + slots) * features,
             transcendentals=0,
         ),
-    )(*args)
+    )(role, *routes, *gates, tokens[0], tokens[1], grads[0], grads[1])
 
 
 def from_wire(wire_ref, out_ref):
@@ -250,44 +301,66 @@
     )(*args)
 
 
-def combine_kernel(wire_ref, *refs):
-    *matrix_refs, own_ref, partner_ref, rows_ref = refs
+def combine_kernel(
+    out_wire_ref, grad_wire_ref, pt_ref, hi_ref, lo_ref, out_own_ref, grad_own_ref, partner_ref,
+    out_rows_ref, grad_rows_ref, perm_ref,
+):
     step = pl.program_id(0)
-    width = wire_ref.shape[1]
-    turned = dot(permutation(False), wire_ref[...]).astype(bf16)
-    at = pl.ds(pl.multiple_of(step * BLOCK, BLOCK), BLOCK)
-    for c in range(CHUNKS):
-        rows_ref[at, c * width : (c + 1) * width] = turned[c * BLOCK : (c + 1) * BLOCK]
+    size, width = BLOCK * CHUNKS, out_wire_ref.shape[1]
+
+    @pl.when(step == 0)
+    def _():
+        perm_ref[...] = permutation(False)
+
+    perm = perm_ref[...]
+    for wire_ref, rows_ref in ((out_wire_ref, out_rows_ref), (grad_wire_ref, grad_rows_ref)):
+        for i in range(PACK // BLOCK):
+            turned = dot(perm, wire_ref[i * size : (i + 1) * size, :]).astype(bf16)
+            at = pl.ds(pl.multiple_of(step * PACK + i * BLOCK, BLOCK), BLOCK)
+            for c in range(CHUNKS):
+                rows_ref[at, c * width : (c + 1) * width] = turned[c * BLOCK : (c + 1) * BLOCK]
 
     @pl.when(step == pl.num_programs(0) - 1)
     def _():
-        count = own_ref.shape[0]
-        rows = rows_ref[...]
-        total = dot(matrix_refs[0][...], rows)
-        for ref in matrix_refs[1:]:
-            total = total + dot(ref[...], rows)
-        own_ref[...] = total[:count].astype(own_ref.dtype)
-        partner_ref[...] = total[count:].astype(partner_ref.dtype)
-
-
-def combine(wire, matrices, slots, rows, features):
-    size = BLOCK * CHUNKS
+        count = out_own_ref.shape[0]
+        for c in range(CHUNKS):
+            at = slice(c * width, (c + 1) * width)
+            rows = out_rows_ref[:, at]
+            total = dot(hi_ref[...], rows) + dot(lo_ref[...], rows)
+            out_own_ref[:, at] = total[:count]
+            partner_ref[0, :, at] = total[count:].astype(bf16)
+            total = dot(pt_ref[...], grad_rows_ref[:, at])
+            grad_own_ref[:, at] = total[:count]
+            partner_ref[1, :, at] = total[count:].astype(bf16)
+
+
+def combine(out_wire, grad_wire, matrices, slots, rows, features):
+    size, width = BLOCK * CHUNKS, features // CHUNKS
+    wire_spec = pl.BlockSpec((PACK * CHUNKS, width), lambda i: (i, 0))
     matrix_spec = pl.BlockSpec((2 * rows, slots), lambda i: (0, 0))
     part_spec = pl.BlockSpec((rows, features), lambda i: (0, 0))
     return pl.pallas_call(
         combine_kernel,
-        grid=(slots // BLOCK,),
-        in_specs=[pl.BlockSpec((size, features // CHUNKS), lambda i: (i, 0))] + [matrix_spec] * len(matrices),
-        out_specs=[part_spec, part_spec],
-        out_shape=[jax.ShapeDtypeStruct((rows, features), f32)] * 2,
-        scratch_shapes=[pltpu.VMEM((slots, features), bf16)],
-        compiler_params=pltpu.CompilerParams(vmem_limit_bytes=VMEM_LIMIT),
+        grid=(slots // PACK,),
+        in_specs=[wire_spec] * 2 + [matrix_spec] * 3,
+        out_specs=[part_spec, part_spec, pl.BlockSpec((2, rows, features), lambda i: (0, 0, 0))],
+        out_shape=[
+            jax.ShapeDtypeStruct((rows, features), f32),
+            jax.ShapeDtypeStruct((rows, features), f32),
+            jax.ShapeDtypeStruct((2, rows, features), bf16),
+        ],
+        scratch_shapes=[
+            pltpu.VMEM((slots, features), bf16),
+            pltpu.VMEM((slots, features), bf16),
+            pltpu.VMEM((size, size), bf16),
+        ],
+        compiler_params=pltpu.CompilerParams(vmem_limit_bytes=SMALL_LIMIT),
         cost_estimate=pl.CostEstimate(
-            flops=2 * slots * (2 * rows * len(matrices) + size) * features,
-            bytes_accessed=2 * slots * features + 16 * rows * features,
+            flops=4 * slots * (3 * rows + size) * features,
+            bytes_accessed=4 * slots * features + 16 * rows * features,
             transcendentals=0,
         ),
-    )(wire, *matrices)
+    )(out_wire, grad_wire, *matrices)
 
 
 def local(tokens, grad_out, routes, gates, gate_weight, up_weight, down_weight):
@@ -304,39 +377,15 @@
     def other(array):
         return lax.ppermute(array, "role", swap)
 
-    route_info = jnp.concatenate([routes.astype(f32), gates], axis=1).T
-    route_other = other(route_info)
-    tokens_other = other(tokens)
-    grad_other = other(grad_out)
-
-    place = np.arange(slots)
-    expand = (place[:, None] // per_chip == np.arange(chips)[None, :]).astype(np.float32)
-    source, number = place % per_chip // cap, place % cap
-    target = np.where(np.arange(2 * rows)[None, :] // rows == source[:, None], number[:, None] + 1, -1)
-    vmem = pl.BlockSpec(memory_space=pltpu.VMEM)
-    p, p_turned, slot_gate, gate_hi, gate_lo = pl.pallas_call(
-        route_kernel,
-        in_specs=[pl.BlockSpec(memory_space=pltpu.SMEM)] + [vmem] * 4,
-        out_specs=[vmem] * 5,
-        out_shape=[
-            jax.ShapeDtypeStruct((slots, 2 * rows), bf16),
-            jax.ShapeDtypeStruct((2 * rows, slots), bf16),
-            jax.ShapeDtypeStruct((slots, 1), f32),
-            jax.ShapeDtypeStruct((2 * rows, slots), bf16),
-            jax.ShapeDtypeStruct((2 * rows, slots), bf16),
-        ],
-    )(role, route_info, route_other, jnp.asarray(expand, bf16), jnp.asarray(target, bf16))
-
-    p_spec = pl.BlockSpec((BLOCK, 2 * rows), lambda i: (i, 0))
-    slot_spec = pl.BlockSpec((BLOCK, 1), lambda i: (i, 0))
-    rows_spec = pl.BlockSpec((rows, features), lambda i: (0, 0))
-    normed_wire = pack(
-        pack_normed_kernel, slots, rows, features, [pltpu.VMEM((2 * rows, features), bf16)],
-        [p_spec, rows_spec, rows_spec], (p, tokens, tokens_other),
-    )
-    grad_wire = pack(
-        pack_grad_kernel, slots, rows, features, [],
-        [p_spec, slot_spec, rows_spec, rows_spec], (p, slot_gate, grad_out, grad_other),
+    route_lanes, gate_lanes = routes.T, gates.T
+    normed_wire, grad_wire, *matrices = pack(
+        role,
+        (route_lanes, other(route_lanes)),
+        (gate_lanes, other(gate_lanes)),
+        (tokens, other(tokens)),
+        (grad_out, other(grad_out)),
+        chips,
+        slots,
     )
 
     def exchange(wire):
@@ -354,14 +403,14 @@
     rows_wire = expert_call(
         backward_kernel, grad_in_wire, (down_local, gate_local, up_local), (hidden_a, hidden_b), slots, features, units
     )
+    rows_wire, _ = lax.optimization_barrier((rows_wire, out_back))
     rows_back = exchange(rows_wire)
 
-    out_own, out_partner = combine(out_back, (gate_hi, gate_lo), slots, rows, features)
+    out_own, grad_own, partner = combine(out_back, rows_back, matrices, slots, rows, features)
+    received = other(partner).astype(f32)
     tokens_wide = tokens.astype(f32)
-    layer_out = (tokens_wide + (out_own + other(out_partner))).astype(bf16)
-
-    grad_own, grad_partner = combine(rows_back, (p_turned,), slots, rows, features)
-    grad_normed = grad_own + other(grad_partner)
+    layer_out = (tokens_wide + (out_own + received[0])).astype(bf16)
+    grad_normed = grad_own + received[1]
     inv_rms = lax.rsqrt(jnp.mean(tokens_wide * tokens_wide, axis=1, keepdims=True) + epsilon)
     projected = jnp.mean(grad_normed * tokens_wide, axis=1, keepdims=True)
     grad_in = grad_out.astype(f32) + inv_rms * grad_normed - tokens_wide * inv_rms**3 * projected

time: 348 us -> 307 us (0.88); the launches traced: 342 us -> 306 us
  blocking collectives: 65.4 us -> 140 us
  waiting for transfers between devices: 115 us -> 51.1 us
  Pallas kernels: 108 us -> 85.9 us
  starting transfers between devices: 45.1 us -> 23.4 us
    all_to_all x1 -> x2, blocking collectives: 65.4 us -> 140 us  [exchange(): lax.all_to_all(parts, 'dev', split_axis=0, concat_axis=0, tiled=True)]
    all_to_all x3 -> x2, waiting for transfers between devices: 110 us -> 44.7 us  [exchange(): lax.all_to_all(parts, 'dev', split_axis=0, concat_axis=0, tiled=True)]
    pallas_call x5 -> x2, Pallas kernels: 46 us -> 23.8 us  [the longest x1 13.4 us: pack(): pl.pallas_call(functools.partial(pack_kernel, chips), grid=(2 * half,), i...]
    all_to_all x3 -> x2, starting transfers between devices: 37.3 us -> 19.2 us  [exchange(): lax.all_to_all(parts, 'dev', split_axis=0, concat_axis=0, tiled=True)]
    ppermute x5, starting transfers between devices: 7.79 us -> 4.19 us  [other(): return lax.ppermute(array, 'role', swap)]
  transfers between devices with their start and end apart: 8 -> 7, of which waited for: 6 -> 4; matrix products, arithmetic and copies ran while one was open for 1% -> 0% of each run, Pallas kernels for 19% -> 20%
where the time goes in v2:
time: 307 us; the launch traced here: 306 us
  blocking collectives  140 us (46%)
  Pallas kernels  85.9 us (28%)
  waiting for transfers between devices  51.1 us (17%)
  starting transfers between devices  23.4 us (8%)
  other arithmetic  3.35 us (1%)
    all_to_all x2, blocking collectives, exchange(): lax.all_to_all(parts, 'dev', split_axis=0, concat_axis=0, tiled=True)  140 us
    pallas_call x2, Pallas kernels, expert_call(): pl.pallas_call(kernel, grid=(tiles + CHUNKS,), in_specs=in_specs, out_spe...  62.1 us
    all_to_all x2, waiting for transfers between devices, exchange(): lax.all_to_all(parts, 'dev', split_axis=0, concat_axis=0, tiled=True)  44.7 us
    all_to_all x2, starting transfers between devices, exchange(): lax.all_to_all(parts, 'dev', split_axis=0, concat_axis=0, tiled=True)  19.2 us
    pallas_call x1, Pallas kernels, pack(): pl.pallas_call(functools.partial(pack_kernel, chips), grid=(2 * half,), i...  13.4 us
    pallas_call x1, Pallas kernels, combine(): pl.pallas_call(combine_kernel, grid=(slots // PACK,), in_specs=[wire_spec...  10.4 us
    ppermute x5, waiting for transfers between devices, other(): return lax.ppermute(array, 'role', swap)  6.44 us
  transfers between devices with their start and end apart: 7, of which 4 were waited for; matrix products, arithmetic and copies ran while one was open for 0% of the time, Pallas kernels for 20%

profile of v2, /device:TPU:1, one launch (start us, length us, event | category | flops | bytes accessed | tf_op | source)
XLA Modules:
  0.0 306.0 jit_solution(397691608197379288)
XLA Ops:
  0.6 1.5 collective-permute-start.3
  2.1 0.1 collective-permute-start.2
  2.2 0.4 collective-permute-start
  2.6 0.1 collective-permute-start.1
  2.7 3.0 collective-permute-done.route_other_ref
  5.8 0.0 collective-permute-done.1.gate_other_ref
  5.8 0.0 collective-permute-done.3.grad_other_ref
  5.8 0.0 copy-start.5
  5.8 0.0 collective-permute-done.2.tokens_other_ref
  5.8 0.0 copy-start.6
  5.8 0.5 copy-done.7
  6.3 0.0 copy-done.8
  6.4 0.3 copy-done.5
  6.7 0.3 copy-done.6
  7.0 13.4 %shard_map.86 = (bf16[2560,896]{1,0:T(8,128)(2,1)}, bf16[2560,896]{1,0:T(8,128)(2,1)}, bf16[256,640]{1,0:T(8,128)(2,1)}, bf16[256,640]{1,0:T(8,128)(2,1)}, bf16[256,640]{1,0:T(8,128)(2,1)}) custom-call(s32[1]{0:T(128)} %bitcast.role_ref, s32[4,128]{1,0:T(4,128)} %bitcast.41, s32[4,128]{1,0:T(4,128)} %copy-done.7, f32[4,128]{1,0:T(4,128)} %bitcast.43, ...), custom_call_target="tpu_custom_call" | custom-call | flops 4697620480 | bytes 12845056 | tf_op jit(solution)/shard_map/pallas_call | solution.py:141
  20.4 67.1 %all_to_all.20 = bf16[64,40,896]{2,1,0:T(8,128)(2,1)} all-to-all(bf16[64,40,896]{2,1,0:T(8,128)(2,1)} %bitcast.30), channel_id=1, replica_groups=mesh['role'=2,'dev'=64] {'dev'}, dimensions={0} | all-to-all | bytes 9175040 | tf_op jit(solution)/shard_map/all_to_all | solution.py:393
  87.5 6.5 %all-to-all-start.2 = ((bf16[64,40,896]{2,1,0:T(8,128)(2,1)}), bf16[64,40,896]{2,1,0:T(8,128)(2,1)}, u32[]{:S(2)}, u32[]{:S(2)}) async-start(bf16[64,40,896]{2,1,0:T(8,128)(2,1)} %bitcast.28), calls=%async_computation.2 | async-start | bytes 9175040 | tf_op jit(solution)/shard_map/all_to_all | solution.py:393
  94.0 30.6 %shard_map.87 = (bf16[2560,896]{1,0:T(8,128)(2,1)}, f32[640,1024]{1,0:T(8,128)}, f32[640,1024]{1,0:T(8,128)}) custom-call(bf16[2560,896]{1,0:T(8,128)(2,1)} %bitcast.31, bf16[3584,1024]{1,0:T(8,128)(2,1)} %bitcast.34, bf16[3584,1024]{1,0:T(8,128)(2,1)} %bitcast.36, bf16[1024,3584]{1,0:T(8,128)(2,1)} %bitcast.38), custom_call_target="tpu_custom_call" | custom-call | flops 18790481920 | bytes 36438016 | tf_op jit(solution)/shard_map/pallas_call | solution.py:288
  124.6 23.2 %all-to-all-done.2 = bf16[64,40,896]{2,1,0:T(8,128)(2,1)} async-done(((bf16[64,40,896]{2,1,0:T(8,128)(2,1)}), bf16[64,40,896]{2,1,0:T(8,128)(2,1)}, u32[]{:S(2)}, u32[]{:S(2)}) %all-to-all-start.2) | async-done | bytes 4587552 | tf_op jit(solution)/shard_map/all_to_all | solution.py:393
  147.9 12.7 %all-to-all-start.1 = ((bf16[64,40,896]{2,1,0:T(8,128)(2,1)}), bf16[64,40,896]{2,1,0:T(8,128)(2,1)}, u32[]{:S(2)}, u32[]{:S(2)}) async-start(bf16[64,40,896]{2,1,0:T(8,128)(2,1)} %bitcast.29), calls=%async_computation.1 | async-start | bytes 9175040 | tf_op jit(solution)/shard_map/all_to_all | solution.py:393
  160.6 31.5 %shard_map.88 = bf16[2560,896]{1,0:T(8,128)(2,1)} custom-call(bf16[2560,896]{1,0:T(8,128)(2,1)} %bitcast.11.wire_ref, f32[640,1024]{1,0:T(8,128)} %get-tuple-element.17.a_ref, f32[640,1024]{1,0:T(8,128)} %get-tuple-element.18.b_ref, bf16[1024,3584]{1,0:T(8,128)(2,1)} %bitcast.39, bf16[3584,1024]{1,0:T(8,128)(2,1)} %bitcast.35, bf16[3584,1024]{1,0:T(8,128)(2,1)} %bitcast.37), custom_call_target="tpu_custom_call" | custom-call | flops 18790481920 | bytes 36438016 | tf_op jit(solution)/shard_map/pallas_call | solution.py:288
  192.1 21.4 %all-to-all-done.1 = bf16[64,40,896]{2,1,0:T(8,128)(2,1)} async-done(((bf16[64,40,896]{2,1,0:T(8,128)(2,1)}), bf16[64,40,896]{2,1,0:T(8,128)(2,1)}, u32[]{:S(2)}, u32[]{:S(2)}) %all-to-all-start.1) | async-done | bytes 4587552 | tf_op jit(solution)/shard_map/all_to_all | solution.py:393
  213.5 72.6 %all_to_all.21 = bf16[64,40,896]{2,1,0:T(8,128)(2,1)} all-to-all(bf16[64,40,896]{2,1,0:T(8,128)(2,1)} %bitcast.33), channel_id=1, replica_groups=mesh['role'=2,'dev'=64] {'dev'}, dimensions={0} | all-to-all | bytes 9175040 | tf_op jit(solution)/shard_map/all_to_all | solution.py:393
  286.1 10.4 %shard_map.89 = (f32[128,3584]{1,0:T(8,128)S(1)}, f32[128,3584]{1,0:T(8,128)S(1)}, bf16[2,128,3584]{2,1,0:T(8,128)(2,1)S(1)}) custom-call(bf16[2560,896]{1,0:T(8,128)(2,1)} %bitcast.9.out_wire_ref, bf16[2560,896]{1,0:T(8,128)(2,1)} %bitcast.32, bf16[256,640]{1,0:T(8,128)(2,1)S(1)} %copy-done, bf16[256,640]{1,0:T(8,128)(2,1)S(1)} %copy-done.1, ...), custom_call_target="tpu_custom_call" | custom-call | flops 5872025600 | bytes 16515072 | tf_op jit(solution)/shard_map/pallas_call | solution.py:342
  296.5 0.0 copy-start.3
  296.5 2.1 collective-permute-start.4
  298.6 3.4 %collective-permute-done.4 = bf16[2,128,3584]{2,1,0:T(8,128)(2,1)S(1)} collective-permute-done((bf16[2,128,3584]{2,1,0:T(8,128)(2,1)S(1)}, bf16[2,128,3584]{2,1,0:T(8,128)(2,1)S(1)}, u32[]{:S(2)}, u32[]{:S(2)}) %collective-permute-start.4) | collective-permute-done | bytes 1835040 | tf_op jit(solution)/shard_map/ppermute | solution.py:378
  302.0 0.4 convert_element_type.16
  302.4 0.0 copy-start.4
  302.4 0.5 fusion.1
  303.0 0.7 copy-done.4
  303.6 2.4 fusion.4
  (10 shorter events, 0.0 us)
Async XLA Ops:
  0.6 5.1 %collective-permute-start.3 = (bf16[128,3584]{1,0:T(8,128)(2,1)}, bf16[128,3584]{1,0:T(8,128)(2,1)S(1)}, u32[]{:S(2)}, u32[]{:S(2)}) collective-permute-start(bf16[128,3584]{1,0:T(8,128)(2,1)} %grad_ref.1), channel_id=1, source_target_pairs={{0,64},{64,0},{1,65},{65,1},{2,66},{66,2},{3,67},{67,3},{4,68},{68... | collective-permute-start | bytes 2752520 | tf_op jit(solution)/shard_map/ppermute | solution.py:378
  2.1 3.7 %collective-permute-start.2 = (bf16[128,3584]{1,0:T(8,128)(2,1)}, bf16[128,3584]{1,0:T(8,128)(2,1)S(1)}, u32[]{:S(2)}, u32[]{:S(2)}) collective-permute-start(bf16[128,3584]{1,0:T(8,128)(2,1)} %tokens_ref.1), channel_id=1, source_target_pairs={{0,64},{64,0},{1,65},{65,1},{2,66},{66,2},{3,67},{67,3},{4,68},{68... | collective-permute-start | bytes 2752520 | tf_op jit(solution)/shard_map/ppermute | solution.py:378
  2.2 3.5 %collective-permute-start = (s32[4,128]{1,0:T(4,128)}, s32[4,128]{1,0:T(4,128)S(1)}, u32[]{:S(2)}, u32[]{:S(2)}) collective-permute-start(s32[4,128]{1,0:T(4,128)} %bitcast.40), channel_id=1, source_target_pairs={{0,64},{64,0},{1,65},{65,1},{2,66},{66,2},{3,67},{67,3},{4,68},{68... | collective-permute-start | bytes 6152 | tf_op jit(solution)/shard_map/ppermute | solution.py:378
  2.6 3.1 %collective-permute-start.1 = (f32[4,128]{1,0:T(4,128)}, f32[4,128]{1,0:T(4,128)S(1)}, u32[]{:S(2)}, u32[]{:S(2)}) collective-permute-start(f32[4,128]{1,0:T(4,128)} %bitcast.42), channel_id=1, source_target_pairs={{0,64},{64,0},{1,65},{65,1},{2,66},{66,2},{3,67},{67,3},{4,68},{68... | collective-permute-start | bytes 6152 | tf_op jit(solution)/shard_map/ppermute | solution.py:378
  5.8 0.6 copy-start.7
  5.8 0.6 copy-start.8
  5.8 0.9 copy-start.5
  5.8 1.2 copy-start.6
  87.5 60.4 %all-to-all-start.2 = ((bf16[64,40,896]{2,1,0:T(8,128)(2,1)}), bf16[64,40,896]{2,1,0:T(8,128)(2,1)}, u32[]{:S(2)}, u32[]{:S(2)}) async-start(bf16[64,40,896]{2,1,0:T(8,128)(2,1)} %bitcast.28), calls=%async_computation.2 | async-start | bytes 9175040 | tf_op jit(solution)/shard_map/all_to_all | solution.py:393
  147.9 65.6 %all-to-all-start.1 = ((bf16[64,40,896]{2,1,0:T(8,128)(2,1)}), bf16[64,40,896]{2,1,0:T(8,128)(2,1)}, u32[]{:S(2)}, u32[]{:S(2)}) async-start(bf16[64,40,896]{2,1,0:T(8,128)(2,1)} %bitcast.29), calls=%async_computation.1 | async-start | bytes 9175040 | tf_op jit(solution)/shard_map/all_to_all | solution.py:393
  213.5 72.6 %copy-start = (bf16[256,640]{1,0:T(8,128)(2,1)S(1)}, bf16[256,640]{1,0:T(8,128)(2,1)}, u32[]{:S(2)}) copy-start(bf16[256,640]{1,0:T(8,128)(2,1)} %get-tuple-element.20.pt_ref) | copy-start | bytes 983044
  213.5 72.6 %copy-start.1 = (bf16[256,640]{1,0:T(8,128)(2,1)S(1)}, bf16[256,640]{1,0:T(8,128)(2,1)}, u32[]{:S(2)}) copy-start(bf16[256,640]{1,0:T(8,128)(2,1)} %get-tuple-element.21.hi_ref) | copy-start | bytes 983044
  213.5 72.6 %copy-start.2 = (bf16[256,640]{1,0:T(8,128)(2,1)S(1)}, bf16[256,640]{1,0:T(8,128)(2,1)}, u32[]{:S(2)}) copy-start(bf16[256,640]{1,0:T(8,128)(2,1)} %get-tuple-element.22.lo_ref) | copy-start | bytes 983044
  296.5 5.9 %copy-start.3 = (bf16[128,3584]{1,0:T(8,128)(2,1)S(1)}, bf16[128,3584]{1,0:T(8,128)(2,1)}, u32[]{:S(2)}) copy-start(bf16[128,3584]{1,0:T(8,128)(2,1)} %tokens_ref.1) | copy-start | bytes 2752516
  296.5 5.5 %collective-permute-start.4 = (bf16[2,128,3584]{2,1,0:T(8,128)(2,1)S(1)}, bf16[2,128,3584]{2,1,0:T(8,128)(2,1)S(1)}, u32[]{:S(2)}, u32[]{:S(2)}) collective-permute-start(bf16[2,128,3584]{2,1,0:T(8,128)(2,1)S(1)} %get-tuple-element.24), channel_id=1, source_target_pairs={{0,64},{64,0},{1,65},{65,1},{2,66},{66,2},{3,67},{67,3},{4,68},{68... | collective-permute-start | bytes 5505032 | tf_op jit(solution)/shard_map/ppermute | solution.py:378
  302.4 1.2 copy-start.4

commit v3 on v2

v3 whole, which is shorter than its diff:
```python
import functools
import math

import jax
import jax.numpy as jnp
from jax import lax
from jax.experimental import pallas as pl
from jax.experimental.pallas import tpu as pltpu
from jax.sharding import PartitionSpec as P

epsilon = 1e-06
bf16, f32 = jnp.bfloat16, jnp.float32
CHUNKS = 4
BLOCK = 64
EARLY = 6
PER_CHIP = 10
AHEAD = 5 * 1024 * 1024
FORWARD_TILE, BACKWARD_TILE = 256, 512
GROUP = 16
VMEM_LIMIT = 60 * 1024 * 1024
SMALL_LIMIT = 40 * 1024 * 1024


def dot(a, b):
    return jnp.dot(a, b, preferred_element_type=f32)


def dot_nt(a, b):
    return lax.dot_general(a, b, (((1,), (1,)), ((), ())), preferred_element_type=f32)


LATE = PER_CHIP - EARLY
UNITS = PER_CHIP + EARLY
SIDE = BLOCK // UNITS
TEN_EARLY, TEN_LATE = SIDE * EARLY, SIDE * LATE


def permutation(to_wire, mixed):
    size = BLOCK * CHUNKS
    wire = lax.broadcasted_iota(jnp.int32, (size, size), 0 if to_wire else 1)
    held = lax.broadcasted_iota(jnp.int32, (size, size), 1 if to_wire else 0)
    unit = lax.shift_right_logical(wire, 2)
    if mixed:
        chip, part = lax.shift_right_logical(unit, 4), unit & (UNITS - 1)
        six = TEN_EARLY + TEN_LATE + chip * EARLY + part - PER_CHIP
        late = TEN_EARLY + chip * LATE + part - EARLY
        unit = jnp.where(part < EARLY, chip * EARLY + part, jnp.where(part < PER_CHIP, late, six))
    return jnp.where((wire & (CHUNKS - 1)) * BLOCK + unit == held, 1.0, 0.0).astype(bf16)


def to_wire(perm, rows, width):
    stacked = jnp.concatenate([rows[:, c * width : (c + 1) * width] for c in range(CHUNKS)], axis=0)
    return dot(perm, stacked).astype(bf16)


def mixed_to_wire(out_ref, base, perm, ten_early, ten_late, six, width):
    size = BLOCK * CHUNKS
    for j in range(six.shape[0] // TEN_EARLY):
        rows = jnp.concatenate(
            [
                ten_early[j * TEN_EARLY : (j + 1) * TEN_EARLY],
                ten_late[j * TEN_LATE : (j + 1) * TEN_LATE],
                six[j * TEN_EARLY : (j + 1) * TEN_EARLY],
            ],
            axis=0,
        ).astype(bf16)
        out_ref[pl.ds(base + j * size, size), :] = to_wire(perm, rows, width)


def mixed_from_wire(wire_ref, base, perm, pair, early, ten_ref, six_ref):
    size, width = BLOCK * CHUNKS, wire_ref.shape[1]
    turned = [dot(perm, wire_ref[pl.ds(base + j * size, size), :]) for j in range(2)]
    edges = (0, TEN_EARLY, TEN_EARLY + TEN_LATE, BLOCK)
    places = (
        (ten_ref, pair * 2 * TEN_EARLY, 2 * TEN_EARLY),
        (ten_ref, early + pair * 2 * TEN_LATE, 2 * TEN_LATE),
        (six_ref, pair * 2 * TEN_EARLY, 2 * TEN_EARLY),
    )
    for n, (ref, start, count) in enumerate(places):
        at = pl.ds(pl.multiple_of(start, 16), count)
        for c in range(CHUNKS):
            rows = [t[c * BLOCK + edges[n] : c * BLOCK + edges[n + 1]] for t in turned]
            ref[at, c * width : (c + 1) * width] = jnp.concatenate(rows, axis=0).astype(bf16)


def plain_from_wire(wire_ref, base, perm, ref, start):
    size, width = BLOCK * CHUNKS, wire_ref.shape[1]
    turned = dot(perm, wire_ref[pl.ds(base, size), :]).astype(bf16)
    at = pl.ds(pl.multiple_of(start, 16), BLOCK)
    for c in range(CHUNKS):
        ref[at, c * width : (c + 1) * width] = turned[c * BLOCK : (c + 1) * BLOCK]


def slot_tables(chips, slots, rows):
    early = chips * EARLY
    cap = PER_CHIP // 2
    slot = lax.broadcasted_iota(jnp.int32, (slots, chips), 0)
    chip = lax.broadcasted_iota(jnp.int32, (slots, chips), 1)
    first = jnp.where(slot < early, chip * EARLY, early + chip * LATE)
    count = jnp.where(slot < early, EARLY, LATE)
    expand = jnp.where((slot >= first) & (slot < first + count), 1.0, 0.0)
    base = jnp.where(slot < early, first, first - EARLY).astype(f32)
    place = slot[:, :1].astype(f32) - jnp.sum(expand * base, axis=1, keepdims=True)
    partner = place >= cap
    rank = jnp.where(partner, place - cap, place) + 1.0
    lane = lax.broadcasted_iota(jnp.int32, (slots, 2 * rows), 1).astype(f32)
    side = jnp.where(partner, 1.0, 0.0)
    target = jnp.where(jnp.where(lane >= rows, 1.0, 0.0) == side, rank, -1.0)
    return expand.astype(bf16), target


def chosen_slots(role, sides, chips, slots):
    top, rows = sides[0][0].shape
    expand, target = slot_tables(chips, slots, rows)
    named = lax.broadcasted_iota(jnp.int32, (chips, rows), 0) + role * chips
    before = lax.broadcasted_iota(jnp.int32, (rows, rows), 0)
    after = lax.broadcasted_iota(jnp.int32, (rows, rows), 1)
    strict = jnp.where(before < after, 1.0, 0.0).astype(bf16)
    ranks, gates = [], []
    for route_ref, gate_ref in sides:
        uses = jnp.zeros((chips, rows), f32)
        gate = jnp.zeros((chips, rows), f32)
        for k in range(top):
            hit = named == route_ref[k : k + 1, :]
            uses = jnp.where(hit, 1.0, uses)
            gate = jnp.where(hit, gate_ref[k : k + 1, :], gate)
        ranks.append(uses * (dot(uses.astype(bf16), strict) + 1.0))
        gates.append(gate)
    rank = jnp.concatenate(ranks, axis=1).astype(bf16)
    gate = jnp.concatenate(gates, axis=1)
    chosen = dot(expand, rank) == target
    first = gate.astype(bf16)
    rest = gate - first.astype(f32)
    second = rest.astype(bf16)
    third = (rest - second.astype(f32)).astype(bf16)
    spread = dot(expand, first) + (dot(expand, second) + dot(expand, third))
    return jnp.where(chosen, 1.0, 0.0), jnp.where(chosen, spread, 0.0)


def route_kernel(
    chips, role_ref, route_ref, route_other_ref, gate_ref, gate_other_ref, p_ref, slot_gate_ref, pt_ref, hi_ref, lo_ref
):
    sides = ((route_ref, gate_ref), (route_other_ref, gate_other_ref))
    one_hot, spread = chosen_slots(role_ref[0], sides, chips, p_ref.shape[0])
    p_ref[...] = one_hot.astype(bf16)
    slot_gate_ref[...] = jnp.sum(spread, axis=1, keepdims=True)
    pt_ref[...] = jnp.transpose(one_hot).astype(bf16)
    turned = jnp.transpose(spread)
    hi = turned.astype(bf16)
    hi_ref[...] = hi
    lo_ref[...] = (turned - hi.astype(f32)).astype(bf16)


def route(role, routes, gates, chips, slots):
    rows = routes[0].shape[1]
    vmem = pl.BlockSpec(memory_space=pltpu.VMEM)
    turned_shape = jax.ShapeDtypeStruct((2 * rows, slots), bf16)
    return pl.pallas_call(
        functools.partial(route_kernel, chips),
        in_specs=[pl.BlockSpec(memory_space=pltpu.SMEM)] + [vmem] * 4,
        out_specs=[vmem] * 5,
        out_shape=[
            jax.ShapeDtypeStruct((slots, 2 * rows), bf16),
            jax.ShapeDtypeStruct((slots, 1), f32),
            turned_shape, turned_shape, turned_shape,
        ],
        compiler_params=pltpu.CompilerParams(vmem_limit_bytes=VMEM_LIMIT),
        cost_estimate=pl.CostEstimate(
            flops=8 * slots * rows * chips, bytes_accessed=12 * slots * rows, transcendentals=0
        ),
    )(role, *routes, *gates)


def pack_kernel(
    p_early_ref, p_late_ref, gate_early_ref, gate_late_ref, tokens_ref, tokens_other_ref, grad_ref, grad_other_ref,
    large_ref, small_ref, normed_ref, mixed_ref, plain_ref,
):
    rows = tokens_ref.shape[0]
    width = large_ref.shape[1]

    @pl.when(pl.program_id(0) == 0)
    def _():
        mixed_ref[...] = permutation(True, True)
        plain_ref[...] = permutation(True, False)
        for i, ref in enumerate((tokens_ref, tokens_other_ref)):
            wide = ref[...].astype(f32)
            inv_rms = lax.rsqrt(jnp.mean(wide * wide, axis=1, keepdims=True) + epsilon)
            normed_ref[i * rows : (i + 1) * rows, :] = (wide * inv_rms).astype(bf16)

    early = p_early_ref.shape[0]
    p = jnp.concatenate([p_early_ref[...], p_late_ref[...]], axis=0)
    gate = jnp.concatenate([gate_early_ref[...], gate_late_ref[...]], axis=0)
    normed = dot(p, normed_ref[...])
    scaled = (dot(p[:, :rows], grad_ref[...]) + dot(p[:, rows:], grad_other_ref[...])) * gate
    mixed_to_wire(large_ref, 0, mixed_ref[...], normed[:early], normed[early:], scaled[:early], width)
    small_ref[...] = to_wire(plain_ref[...], scaled[early:].astype(bf16), width)


def pack(p, slot_gate, tokens, grads, chips, slots):
    rows, features = tokens[0].shape
    width = features // CHUNKS
    late = chips * EARLY // (GROUP * LATE)
    size = BLOCK * CHUNKS
    rows_spec = pl.BlockSpec((rows, features), lambda i: (0, 0))
    large, small = GROUP * UNITS * CHUNKS, GROUP * LATE * CHUNKS
    steps = chips // GROUP
    return pl.pallas_call(
        pack_kernel,
        grid=(steps,),
        in_specs=[
            pl.BlockSpec((GROUP * EARLY, 2 * rows), lambda i: (i, 0)),
            pl.BlockSpec((GROUP * LATE, 2 * rows), lambda i: (late + i, 0)),
            pl.BlockSpec((GROUP * EARLY, 1), lambda i: (i, 0)),
            pl.BlockSpec((GROUP * LATE, 1), lambda i: (late + i, 0)),
        ]
        + [rows_spec] * 4,
        out_specs=[
            pl.BlockSpec((large, width), lambda i: (i, 0)),
            pl.BlockSpec((small, width), lambda i: (i, 0)),
        ],
        out_shape=[
            jax.ShapeDtypeStruct((steps * large, width), bf16),
            jax.ShapeDtypeStruct((steps * small, width), bf16),
        ],
        scratch_shapes=[
            pltpu.VMEM((2 * rows, features), bf16),
            pltpu.VMEM((size, size), bf16),
            pltpu.VMEM((size, size), bf16),
        ],
        compiler_params=pltpu.CompilerParams(vmem_limit_bytes=VMEM_LIMIT),
        cost_estimate=pl.CostEstimate(
            flops=4 * slots * (2 * rows + size) * features,
            bytes_accessed=4 * (2 * rows + slots) * features,
            transcendentals=0,
        ),
    )(p, p, slot_gate, slot_gate, *tokens, *grads)


class Copies:
    def __init__(self, sems):
        self.sems, self.made = sems, 0
        self.queue, self.flying, self.flying_bytes = [], [], 0

    def start(self, source, target):
        copy = pltpu.make_async_copy(source, target, self.sems.at[self.made])
        self.made += 1
        copy.start()
        return copy

    def add(self, source, target):
        self.queue.append((source, target, math.prod(target.shape) * target.dtype.itemsize))

    def fill(self):
        while self.queue and self.flying_bytes < AHEAD:
            source, target, size = self.queue.pop(0)
            self.flying.append((self.start(source, target), size))
            self.flying_bytes += size

    def take(self, count=1):
        for _ in range(count):
            self.fill()
            copy, size = self.flying.pop(0)
            copy.wait()
            self.flying_bytes -= size
        self.fill()


def tile_of(n, size):
    return slice(n * size, (n + 1) * size)


def forward_kernel(
    large_hbm, gate_hbm, up_hbm, down_hbm, small_hbm, out_early_hbm, grad_early_hbm, a_hbm, b_hbm,
    large_ref, gate_ref, up_ref, down_ref, x_ref, grad_early_ref, product_ref, a_ref, b_ref, out_early_ref, small_ref,
    sems,
):
    size, width = BLOCK * CHUNKS, small_ref.shape[1]
    pairs, tiles = large_ref.shape[0] // (2 * size), gate_ref.shape[1] // FORWARD_TILE
    early = out_early_ref.shape[0]
    copies = Copies(sems)
    for i in range(pairs):
        copies.add(large_hbm.at[tile_of(i, 2 * size)], large_ref.at[tile_of(i, 2 * size)])
    for n in range(tiles):
        for source, target in ((gate_hbm, gate_ref), (up_hbm, up_ref)):
            copies.add(source.at[:, tile_of(n, FORWARD_TILE)], target.at[:, tile_of(n, FORWARD_TILE)])
    for c in range(CHUNKS):
        copies.add(down_hbm.at[:, tile_of(c, width)], down_ref.at[:, tile_of(c, width)])
    copies.fill()
    out = []

    perm = permutation(False, True)
    for i in range(pairs):
        copies.take()
        mixed_from_wire(large_ref, i * 2 * size, perm, i, early, x_ref, grad_early_ref)
    out.append(copies.start(grad_early_ref, grad_early_hbm))

    for n in range(tiles):
        copies.take(2)
        at = tile_of(n, FORWARD_TILE)
        hidden_a = dot(x_ref[...], gate_ref[:, at])
        hidden_b = dot(x_ref[...], up_ref[:, at])
        a_ref[:, at] = hidden_a
        b_ref[:, at] = hidden_b
        product_ref[:, at] = (hidden_a * jax.nn.sigmoid(hidden_a) * hidden_b).astype(bf16)
        out.append(copies.start(a_ref.at[:, at], a_hbm.at[:, at]))
        out.append(copies.start(b_ref.at[:, at], b_hbm.at[:, at]))

    for c in range(CHUNKS):
        copies.take()
        at = tile_of(c, width)
        rows = dot(product_ref[...], down_ref[:, at]).astype(bf16)
        out_early_ref[:, at] = rows[:early]
        x_ref[early:, at] = rows[early:]
        out.append(copies.start(out_early_ref.at[:, at], out_early_hbm.at[:, at]))

    perm = permutation(True, False)
    for i in range(small_ref.shape[0] // size):
        at = tile_of(i, size)
        small_ref[at, :] = to_wire(perm, x_ref[early + i * BLOCK : early + (i + 1) * BLOCK, :], width)
        out.append(copies.start(small_ref.at[at], small_hbm.at[at]))
    for copy in out:
        copy.wait()


def backward_kernel(
    small_hbm, grad_early_hbm, out_early_hbm, a_hbm, b_hbm, down_hbm, gate_hbm, up_hbm, large_hbm,
    small_ref, out_early_ref, a_ref, b_ref, down_ref, gate_ref, up_ref, x_ref, grad_a_ref, grad_b_ref, large_ref,
    sems,
):
    size, width = BLOCK * CHUNKS, large_ref.shape[1]
    pairs, tiles = large_ref.shape[0] // (2 * size), gate_ref.shape[1] // BACKWARD_TILE
    early = out_early_ref.shape[0]
    copies = Copies(sems)
    copies.add(small_hbm, small_ref)
    copies.add(grad_early_hbm, x_ref.at[:early])
    for n in range(tiles):
        at = tile_of(n, BACKWARD_TILE)
        copies.add(down_hbm.at[at], down_ref.at[at])
        copies.add(a_hbm.at[:, at], a_ref.at[:, at])
        copies.add(b_hbm.at[:, at], b_ref.at[:, at])
    for c in range(CHUNKS):
        at = tile_of(c, width)
        copies.add(gate_hbm.at[at], gate_ref.at[at])
        copies.add(up_hbm.at[at], up_ref.at[at])
    copies.add(out_early_hbm, out_early_ref)
    copies.fill()

    perm = permutation(False, False)
    copies.take()
    for i in range(small_ref.shape[0] // size):
        plain_from_wire(small_ref, i * size, perm, x_ref, early + i * BLOCK)
    copies.take()

    for n in range(tiles):
        copies.take(3)
        at = tile_of(n, BACKWARD_TILE)
        grad_act = dot_nt(x_ref[...], down_ref[at, :])
        hidden_a, hidden_b = a_ref[:, at], b_ref[:, at]
        sigmoid_a = jax.nn.sigmoid(hidden_a)
        slope = sigmoid_a * (1.0 + hidden_a * (1.0 - sigmoid_a))
        grad_a_ref[:, at] = (grad_act * hidden_b * slope).astype(bf16)
        grad_b_ref[:, at] = (grad_act * (hidden_a * sigmoid_a)).astype(bf16)

    for c in range(CHUNKS):
        copies.take(2)
        at = tile_of(c, width)
        rows = dot_nt(grad_a_ref[...], gate_ref[at, :]) + dot_nt(grad_b_ref[...], up_ref[at, :])
        x_ref[:, at] = rows.astype(bf16)

    copies.take()
    perm = permutation(True, True)
    out = []
    for i in range(pairs):
        ten, late = 2 * TEN_EARLY, 2 * TEN_LATE
        mixed_to_wire(
            large_ref,
            i * 2 * size,
            perm,
            x_ref[i * ten : (i + 1) * ten, :].astype(f32),
            x_ref[early + i * late : early + (i + 1) * late, :].astype(f32),
            out_early_ref[i * ten : (i + 1) * ten, :].astype(f32),
            width,
        )
        out.append(copies.start(large_ref.at[tile_of(i, 2 * size)], large_hbm.at[tile_of(i, 2 * size)]))
    for copy in out:
        copy.wait()


def expert_call(forward, args, slots, features, units):
    tiles = units // (FORWARD_TILE if forward else BACKWARD_TILE)
    width, size = features // CHUNKS, BLOCK * CHUNKS
    early = slots * EARLY // PER_CHIP
    large, small = slots * UNITS * CHUNKS // PER_CHIP, (slots - early) * CHUNKS
    pairs = large // (2 * size)

    def shape(*dims, dtype=bf16):
        return jax.ShapeDtypeStruct(dims, dtype)

    hidden = (slots, units)
    scratch = {
        "large": pltpu.VMEM((large, width), bf16),
        "small": pltpu.VMEM((small, width), bf16),
        "early": pltpu.VMEM((early, features), bf16),
        "x": pltpu.VMEM((slots, features), bf16),
        "wide": pltpu.VMEM(hidden, f32),
        "narrow": pltpu.VMEM(hidden, bf16),
        "up": pltpu.VMEM((features, units), bf16),
        "down": pltpu.VMEM((units, features), bf16),
    }
    if forward:
        kernel = forward_kernel
        out_shape = [
            shape(small, width), shape(early, features), shape(early, features),
            shape(*hidden, dtype=f32), shape(*hidden, dtype=f32),
        ]
        names = ("large", "up", "up", "down", "x", "early", "narrow", "wide", "wide", "early", "small")
        count = pairs + 4 * tiles + 1 + 2 * CHUNKS + small // size
    else:
        kernel = backward_kernel
        out_shape = shape(large, width)
        names = ("small", "early", "wide", "wide", "down", "up", "up", "x", "narrow", "narrow", "large")
        count = 3 + 3 * tiles + 2 * CHUNKS + pairs
    hbm = pl.BlockSpec(memory_space=pl.ANY)
    return pl.pallas_call(
        kernel,
        in_specs=[hbm] * len(args),
        out_specs=jax.tree.map(lambda _: hbm, out_shape),
        out_shape=out_shape,
        scratch_shapes=[scratch[name] for name in names] + [pltpu.SemaphoreType.DMA((count,))],
        compiler_params=pltpu.CompilerParams(vmem_limit_bytes=VMEM_LIMIT),
        cost_estimate=pl.CostEstimate(
            flops=6 * slots * units * features,
            bytes_accessed=6 * units * features + 6 * slots * features + 8 * slots * units,
            transcendentals=slots * units,
        ),
    )(*args)


def combine_kernel(
    small_ref, large_ref, pt_ref, hi_ref, lo_ref, out_own_ref, grad_own_ref, partner_ref,
    out_rows_ref, grad_rows_ref, mixed_ref, plain_ref,
):
    step = pl.program_id(0)
    size, width = BLOCK * CHUNKS, large_ref.shape[1]
    early = out_rows_ref.shape[0] * EARLY // PER_CHIP

    @pl.when(step == 0)
    def _():
        mixed_ref[...] = permutation(False, True)
        plain_ref[...] = permutation(False, False)

    pairs = large_ref.shape[0] // (2 * size)
    for i in range(pairs):
        mixed_from_wire(large_ref, i * 2 * size, mixed_ref[...], step * pairs + i, early, grad_rows_ref, out_rows_ref)
    for i in range(small_ref.shape[0] // size):
        start = early + step * (small_ref.shape[0] // CHUNKS) + i * BLOCK
        plain_from_wire(small_ref, i * size, plain_ref[...], out_rows_ref, start)

    @pl.when(step == pl.num_programs(0) - 1)
    def _():
        count = out_own_ref.shape[0]
        for c in range(CHUNKS):
            at = slice(c * width, (c + 1) * width)
            rows = out_rows_ref[:, at]
            total = dot(hi_ref[...], rows) + dot(lo_ref[...], rows)
            out_own_ref[:, at] = total[:count]
            partner_ref[0, :, at] = total[count:].astype(bf16)
            total = dot(pt_ref[...], grad_rows_ref[:, at])
            grad_own_ref[:, at] = total[:count]
            partner_ref[1, :, at] = total[count:].astype(bf16)


def combine(small, large, matrices, slots, rows, features):
    size, width = BLOCK * CHUNKS, features // CHUNKS
    steps = small.shape[0] // (GROUP * LATE * CHUNKS)
    matrix_spec = pl.BlockSpec((2 * rows, slots), lambda i: (0, 0))
    part_spec = pl.BlockSpec((rows, features), lambda i: (0, 0))
    return pl.pallas_call(
        combine_kernel,
        grid=(steps,),
        in_specs=[
            pl.BlockSpec((GROUP * LATE * CHUNKS, width), lambda i: (i, 0)),
            pl.BlockSpec((GROUP * UNITS * CHUNKS, width), lambda i: (i, 0)),
        ]
        + [matrix_spec] * 3,
        out_specs=[part_spec, part_spec, pl.BlockSpec((2, rows, features), lambda i: (0, 0, 0))],
        out_shape=[
            jax.ShapeDtypeStruct((rows, features), f32),
            jax.ShapeDtypeStruct((rows, features), f32),
            jax.ShapeDtypeStruct((2, rows, features), bf16),
        ],
        scratch_shapes=[
            pltpu.VMEM((slots, features), bf16),
            pltpu.VMEM((slots, features), bf16),
            pltpu.VMEM((size, size), bf16),
            pltpu.VMEM((size, size), bf16),
        ],
        compiler_params=pltpu.CompilerParams(vmem_limit_bytes=SMALL_LIMIT),
        cost_estimate=pl.CostEstimate(
            flops=4 * slots * (3 * rows + size) * features,
            bytes_accessed=4 * slots * features + 16 * rows * features,
            transcendentals=0,
        ),
    )(small, large, *matrices)


def local(tokens, grad_out, routes, gates, gate_weight, up_weight, down_weight):
    rows, features = tokens.shape
    units = gate_weight.shape[2]
    chips = lax.axis_size("dev")
    slots = chips * PER_CHIP
    role = lax.axis_index("role").astype(jnp.int32).reshape(1)
    swap = [(0, 1), (1, 0)]

    def other(array):
        return lax.ppermute(array, "role", swap)

    def exchange(wire):
        parts = wire.reshape(chips, wire.shape[0] // chips, wire.shape[1])
        parts = lax.all_to_all(parts, "dev", split_axis=0, concat_axis=0, tiled=True)
        return parts.reshape(wire.shape)

    route_lanes, gate_lanes = routes.T, gates.T
    route_other, gate_other = other(route_lanes), other(gate_lanes)
    p, slot_gate, *matrices = route(role, (route_lanes, route_other), (gate_lanes, gate_other), chips, slots)
    late_grad, _, _ = lax.optimization_barrier((grad_out, route_other, gate_other))
    large, small = pack(p, slot_gate, (tokens, other(tokens)), (grad_out, other(late_grad)), chips, slots)
    gate_local, up_local, down_local = gate_weight[0], up_weight[0], down_weight[0]

    large_in = exchange(large)
    small, _ = lax.optimization_barrier((small, large_in))
    small_in = exchange(small)
    small_out, out_early, grad_early, hidden_a, hidden_b = expert_call(
        True, (large_in, gate_local, up_local, down_local), slots, features, units
    )
    small_back = exchange(small_out)
    large_out = expert_call(
        False,
        (small_in, grad_early, out_early, hidden_a, hidden_b, down_local, gate_local, up_local),
        slots, features, units,
    )
    large_out, _ = lax.optimization_barrier((large_out, small_back))
    large_back = exchange(large_out)

    out_own, grad_own, partner = combine(small_back, large_back, matrices, slots, rows, features)
    received = other(partner).astype(f32)
    tokens_wide = tokens.astype(f32)
    layer_out = (tokens_wide + (out_own + received[0])).astype(bf16)
    grad_normed = grad_own + received[1]
    inv_rms = lax.rsqrt(jnp.mean(tokens_wide * tokens_wide, axis=1, keepdims=True) + epsilon)
    projected = jnp.mean(grad_normed * tokens_wide, axis=1, keepdims=True)
    grad_in = grad_out.astype(f32) + inv_rms * grad_normed - tokens_wide * inv_rms**3 * projected
    return (layer_out, grad_in.astype(bf16))


def solution(mesh):
    split = P(("role", "dev"), None)
    split_weight = P(("role", "dev"), None, None)
    in_specs = (split, split, split, split, split_weight, split_weight, split_weight)
    return jax.shard_map(local, mesh=mesh, in_specs=in_specs, out_specs=(split, split), check_vma=False)
```

time: 307 us -> 305 us (level); the launches traced: 306 us -> 299 us
  blocking collectives: 140 us -> 189 us
  waiting for transfers between devices: 51.1 us -> 5.03 us
  Pallas kernels: 85.9 us -> 74.1 us
    all_to_all x2, blocking collectives: 140 us -> 189 us  [exchange(): lax.all_to_all(parts, 'dev', split_axis=0, concat_axis=0, tiled=True)]
    all_to_all x2, waiting for transfers between devices: 44.7 us -> 0.76 us  [exchange(): lax.all_to_all(parts, 'dev', split_axis=0, concat_axis=0, tiled=True)]
    pallas_call x4 -> x5, Pallas kernels: 85.9 us -> 74.1 us  [the longest x2 48.8 us: expert_call(): pl.pallas_call(kernel, in_specs=[hbm] * len(args), out_specs=jax.tree.map...]
  transfers between devices with their start and end apart: 7 -> 7, of which waited for: 4 -> 4; matrix products, arithmetic and copies ran while one was open for 0% -> 0% of each run, Pallas kernels for 20% -> 17%
where the time goes in v3:
time: 305 us; the launch traced here: 299 us
  blocking collectives  189 us (62%)
  Pallas kernels  74.1 us (24%)
  starting transfers between devices  23.1 us (8%)
  waiting for transfers between devices  5.03 us (2%)
  local copies, waits for them, and re-layouts  3.51 us (1%)
  other arithmetic  3.35 us (1%)
    all_to_all x2, blocking collectives, exchange(): lax.all_to_all(parts, 'dev', split_axis=0, concat_axis=0, tiled=True)  189 us
    pallas_call x2, Pallas kernels, expert_call(): pl.pallas_call(kernel, in_specs=[hbm] * len(args), out_specs=jax.tree.map...  48.8 us
    all_to_all x2, starting transfers between devices, exchange(): lax.all_to_all(parts, 'dev', split_axis=0, concat_axis=0, tiled=True)  16.9 us
    pallas_call x1, Pallas kernels, pack(): pl.pallas_call(pack_kernel, grid=(steps,), in_specs=[pl.BlockSpec((GROUP...  11.8 us
    pallas_call x1, Pallas kernels, combine(): pl.pallas_call(combine_kernel, grid=(steps,), in_specs=[pl.BlockSpec((GRO...  10.8 us
    ppermute x5, starting transfers between devices, other(): return lax.ppermute(array, 'role', swap)  6.24 us
  transfers between devices with their start and end apart: 7, of which 4 were waited for; matrix products, arithmetic and copies ran while one was open for 0% of the time, Pallas kernels for 17%

profile of v3, /device:TPU:1, one launch (start us, length us, event | category | flops | bytes accessed | tf_op | source)
XLA Modules:
  0.0 298.9 jit_solution(14713561249605965680)
XLA Ops:
  0.6 1.5 collective-permute-start
  2.1 0.1 collective-permute-start.1
  2.2 0.4 collective-permute-start.2
  2.6 0.5 collective-permute-done.route_other_ref
  3.2 0.3 collective-permute-done.1.gate_other_ref
  3.5 0.2 collective-permute-start.3
  3.7 0.1 copy-done.8
  3.7 0.3 copy-done.9
  4.1 2.8 shard_map.86
  6.8 0.0 collective-permute-done.2.tokens_other_ref
  6.8 0.0 collective-permute-done.3.grad_other_ref
  6.9 0.0 copy-start.7
  6.9 0.9 copy-done.6
  7.8 0.3 copy-done.7
  8.1 11.8 %shard_map.87 = (bf16[4096,896]{1,0:T(8,128)(2,1)}, bf16[1024,896]{1,0:T(8,128)(2,1)}) custom-call(bf16[640,256]{1,0:T(8,128)(2,1)} %get-tuple-element.20.p_early_ref.p_late_ref, bf16[640,256]{1,0:T(8,128)(2,1)} %get-tuple-element.20.p_early_ref.p_late_ref, f32[640,1]{1,0:T(8,128)} %get-tuple-element.21.gate_early_ref.gate_late_ref, ...), custom_call_target="tpu_custom_call" | custom-call | flops 4697620480 | bytes 12845056 | tf_op jit(solution)/shard_map/pallas_call | solution.py:207
  19.9 95.9 %all_to_all.20 = bf16[64,64,896]{2,1,0:T(8,128)(2,1)} all-to-all(bf16[64,64,896]{2,1,0:T(8,128)(2,1)} %bitcast.32), channel_id=1, replica_groups=mesh['role'=2,'dev'=64] {'dev'}, dimensions={0} | all-to-all | bytes 14680064 | tf_op jit(solution)/shard_map/all_to_all | solution.py:520
  115.8 7.8 %all-to-all-start.2 = ((bf16[64,16,896]{2,1,0:T(8,128)(2,1)}), bf16[64,16,896]{2,1,0:T(8,128)(2,1)S(1)}, u32[]{:S(2)}, u32[]{:S(2)}) async-start(bf16[64,16,896]{2,1,0:T(8,128)(2,1)} %bitcast.34), calls=%async_computation.2 | async-start | bytes 3670016 | tf_op jit(solution)/shard_map/all_to_all | solution.py:520
  123.6 23.3 %shard_map.88 = (bf16[1024,896]{1,0:T(8,128)(2,1)}, bf16[384,3584]{1,0:T(8,128)(2,1)}, bf16[384,3584]{1,0:T(8,128)(2,1)}, f32[640,1024]{1,0:T(8,128)}, f32[640,1024]{1,0:T(8,128)}) custom-call(bf16[4096,896]{1,0:T(8,128)(2,1)} %bitcast.29, bf16[3584,1024]{1,0:T(8,128)(2,1)} %bitcast.36, bf16[3584,1024]{1,0:T(8,128)(2,1)} %bitcast.38, bf16[1024,3584]{1,0:T(8,128)(2,1)} %bitcast.40), custom_call_target="tpu_custom_call" | custom-call | flops 14092861440 | bytes 41025536 | tf_op jit(solution)/shard_map/pallas_call | solution.py:424
  146.9 0.8 all-to-all-done.2
  147.7 1.2 copy-done.4
  148.9 9.0 %all-to-all-start.1 = ((bf16[64,16,896]{2,1,0:T(8,128)(2,1)}), bf16[64,16,896]{2,1,0:T(8,128)(2,1)S(1)}, u32[]{:S(2)}, u32[]{:S(2)}) async-start(bf16[64,16,896]{2,1,0:T(8,128)(2,1)} %bitcast.35), calls=%async_computation.1 | async-start | bytes 3670016 | tf_op jit(solution)/shard_map/all_to_all | solution.py:520
  157.9 25.5 %shard_map.89 = bf16[4096,896]{1,0:T(8,128)(2,1)} custom-call(bf16[1024,896]{1,0:T(8,128)(2,1)} %bitcast.33, bf16[384,3584]{1,0:T(8,128)(2,1)} %get-tuple-element.27.grad_early_hbm, bf16[384,3584]{1,0:T(8,128)(2,1)} %get-tuple-element.28.out_early_hbm, f32[640,1024]{1,0:T(8,128)} %get-tuple-element.29.a_hbm, f32[640,1024]{1,0:T(8,128)} %get-tuple-element.30.b_hbm, ...), custom_call_target="tpu_custom_call" | custom-call | flops 14092861440 | bytes 41025536 | tf_op jit(solution)/shard_map/pallas_call | solution.py:424
  183.4 93.0 %all_to_all.21 = bf16[64,64,896]{2,1,0:T(8,128)(2,1)} all-to-all(bf16[64,64,896]{2,1,0:T(8,128)(2,1)} %bitcast.30), channel_id=1, replica_groups=mesh['role'=2,'dev'=64] {'dev'}, dimensions={0} | all-to-all | bytes 14680064 | tf_op jit(solution)/shard_map/all_to_all | solution.py:520
  276.4 10.8 %shard_map.90 = (f32[128,3584]{1,0:T(8,128)S(1)}, f32[128,3584]{1,0:T(8,128)S(1)}, bf16[2,128,3584]{2,1,0:T(8,128)(2,1)S(1)}) custom-call(bf16[1024,896]{1,0:T(8,128)(2,1)S(1)} %bitcast.28, bf16[4096,896]{1,0:T(8,128)(2,1)} %bitcast.31, bf16[256,640]{1,0:T(8,128)(2,1)S(1)} %copy-done, bf16[256,640]{1,0:T(8,128)(2,1)S(1)} %copy-done.1, ...), custom_call_target="tpu_custom_call" | custom-call | flops 5872025600 | bytes 16515072 | tf_op jit(solution)/shard_map/pallas_call | solution.py:478
  287.2 0.0 copy-start.3
  287.2 4.1 %collective-permute-start.4 = (bf16[2,128,3584]{2,1,0:T(8,128)(2,1)S(1)}, bf16[2,128,3584]{2,1,0:T(8,128)(2,1)S(1)}, u32[]{:S(2)}, u32[]{:S(2)}) collective-permute-start(bf16[2,128,3584]{2,1,0:T(8,128)(2,1)S(1)} %get-tuple-element.36), channel_id=1, source_target_pairs={{0,64},{64,0},{1,65},{65,1},{2,66},{66,2},{3,67},{67,3},{4,68},{68... | collective-permute-start | bytes 5505032 | tf_op jit(solution)/shard_map/ppermute | solution.py:516
  291.2 3.4 %collective-permute-done.4 = bf16[2,128,3584]{2,1,0:T(8,128)(2,1)S(1)} collective-permute-done((bf16[2,128,3584]{2,1,0:T(8,128)(2,1)S(1)}, bf16[2,128,3584]{2,1,0:T(8,128)(2,1)S(1)}, u32[]{:S(2)}, u32[]{:S(2)}) %collective-permute-start.4) | collective-permute-done | bytes 1835040 | tf_op jit(solution)/shard_map/ppermute | solution.py:516
  294.6 0.4 convert_element_type.16
  295.1 0.0 copy-start.5
  295.1 0.5 fusion.1
  295.6 0.7 copy-done.5
  296.3 2.4 fusion.4
  (13 shorter events, 0.0 us)
Async XLA Ops:
  0.6 2.5 collective-permute-start
  2.1 1.4 collective-permute-start.1
  2.2 4.6 %collective-permute-start.2 = (bf16[128,3584]{1,0:T(8,128)(2,1)}, bf16[128,3584]{1,0:T(8,128)(2,1)S(1)}, u32[]{:S(2)}, u32[]{:S(2)}) collective-permute-start(bf16[128,3584]{1,0:T(8,128)(2,1)} %tokens_ref.1), channel_id=1, source_target_pairs={{0,64},{64,0},{1,65},{65,1},{2,66},{66,2},{3,67},{67,3},{4,68},{68... | collective-permute-start | bytes 2752520 | tf_op jit(solution)/shard_map/ppermute | solution.py:516
  3.2 0.6 copy-start.8
  3.5 0.6 copy-start.9
  3.5 3.3 %collective-permute-start.3 = (bf16[128,3584]{1,0:T(8,128)(2,1)}, bf16[128,3584]{1,0:T(8,128)(2,1)S(1)}, u32[]{:S(2)}, u32[]{:S(2)}) collective-permute-start(bf16[128,3584]{1,0:T(8,128)(2,1)} %grad_ref.1), channel_id=1, source_target_pairs={{0,64},{64,0},{1,65},{65,1},{2,66},{66,2},{3,67},{67,3},{4,68},{68... | collective-permute-start | bytes 2752520 | tf_op jit(solution)/shard_map/ppermute | solution.py:516
  6.8 0.9 copy-start.6
  6.9 1.2 copy-start.7
  115.8 31.9 %all-to-all-start.2 = ((bf16[64,16,896]{2,1,0:T(8,128)(2,1)}), bf16[64,16,896]{2,1,0:T(8,128)(2,1)S(1)}, u32[]{:S(2)}, u32[]{:S(2)}) async-start(bf16[64,16,896]{2,1,0:T(8,128)(2,1)} %bitcast.34), calls=%async_computation.2 | async-start | bytes 3670016 | tf_op jit(solution)/shard_map/all_to_all | solution.py:520
  147.7 1.2 copy-start.4
  148.9 34.5 %all-to-all-start.1 = ((bf16[64,16,896]{2,1,0:T(8,128)(2,1)}), bf16[64,16,896]{2,1,0:T(8,128)(2,1)S(1)}, u32[]{:S(2)}, u32[]{:S(2)}) async-start(bf16[64,16,896]{2,1,0:T(8,128)(2,1)} %bitcast.35), calls=%async_computation.1 | async-start | bytes 3670016 | tf_op jit(solution)/shard_map/all_to_all | solution.py:520
  183.4 93.0 %copy-start = (bf16[256,640]{1,0:T(8,128)(2,1)S(1)}, bf16[256,640]{1,0:T(8,128)(2,1)}, u32[]{:S(2)}) copy-start(bf16[256,640]{1,0:T(8,128)(2,1)} %get-tuple-element.32.pt_ref) | copy-start | bytes 983044
  183.4 93.0 %copy-start.1 = (bf16[256,640]{1,0:T(8,128)(2,1)S(1)}, bf16[256,640]{1,0:T(8,128)(2,1)}, u32[]{:S(2)}) copy-start(bf16[256,640]{1,0:T(8,128)(2,1)} %get-tuple-element.33.hi_ref) | copy-start | bytes 983044
  183.4 93.0 %copy-start.2 = (bf16[256,640]{1,0:T(8,128)(2,1)S(1)}, bf16[256,640]{1,0:T(8,128)(2,1)}, u32[]{:S(2)}) copy-start(bf16[256,640]{1,0:T(8,128)(2,1)} %get-tuple-element.34.lo_ref) | copy-start | bytes 983044
  287.2 7.9 %copy-start.3 = (bf16[128,3584]{1,0:T(8,128)(2,1)S(1)}, bf16[128,3584]{1,0:T(8,128)(2,1)}, u32[]{:S(2)}) copy-start(bf16[128,3584]{1,0:T(8,128)(2,1)} %tokens_ref.1) | copy-start | bytes 2752516
  287.2 7.5 %collective-permute-start.4 = (bf16[2,128,3584]{2,1,0:T(8,128)(2,1)S(1)}, bf16[2,128,3584]{2,1,0:T(8,128)(2,1)S(1)}, u32[]{:S(2)}, u32[]{:S(2)}) collective-permute-start(bf16[2,128,3584]{2,1,0:T(8,128)(2,1)S(1)} %get-tuple-element.36), channel_id=1, source_target_pairs={{0,64},{64,0},{1,65},{65,1},{2,66},{66,2},{3,67},{67,3},{4,68},{68... | collective-permute-start | bytes 5505032 | tf_op jit(solution)/shard_map/ppermute | solution.py:516
  295.1 1.2 copy-start.5
